TPU v7x, 128 devices: a whole 4x4x4 slice. The times are simulated.
128 devices in a mesh: dp: 8 (over y_hi, z), ctx: 16 (over x, y_lo, core).
Axes of the slice: x: 4, y: 4 (y_hi: 2, y_lo: 2; y = y_hi * 2 + y_lo), z: 4, core: 2. Of those that a mesh axis runs over, the one named last changes fastest.
Arguments:
- xs: bfloat16 [8, 3072, 4096], P('dp', 'ctx'), may hold values from -6 to 6
- z_gate: bfloat16 [8, 3072, 4096], P('dp', 'ctx'), may hold values from -6 to 6
- b_proj: bfloat16 [8, 3072, 256], P('dp', 'ctx'), may hold values from -3 to 3
- c_proj: bfloat16 [8, 3072, 256], P('dp', 'ctx'), may hold values from -3 to 3
- dt_raw: bfloat16 [8, 3072, 64], P('dp', 'ctx'), may hold values from -2.5 to 7.5
- a_log: float32 [64], replicated
- dt_bias: float32 [64], replicated, may hold values from -0.5 to 0.5
- d_skip: float32 [64], replicated, may hold values from 0.5 to 1.5
- norm_gain: float32 [4096], replicated, may hold values from 0.25 to 1.75
- w_out: bfloat16 [4096, 2048], P('dp'), may hold values from -0.09375 to 0.09375
- cotangent: bfloat16 [8, 3072, 2048], P('dp', 'ctx'), may hold values from -6 to 6
Outputs:
- layer_out: bfloat16 [8, 3072, 2048], P('dp', 'ctx')
- grad_xs: bfloat16 [8, 3072, 4096], P('dp', 'ctx')
- grad_gate: bfloat16 [8, 3072, 4096], P('dp', 'ctx')
- grad_b: bfloat16 [8, 3072, 256], P('dp', 'ctx')
- grad_c: bfloat16 [8, 3072, 256], P('dp', 'ctx')
- grad_dt: bfloat16 [8, 3072, 64], P('dp', 'ctx')
- grad_w_out: float32 [4096, 2048], P('dp')
All inputs are finite; a program needn't handle non-finite values.
Results may differ from a plain program's by a relative error of at most 0.012.
Values may be sent and summed in bfloat16 or wider, within the bound.
A program may use at most 384 MiB of HBM per device.

v0:
```python
import math

import jax
import jax.numpy as jnp
from jax import lax
from jax.sharding import PartitionSpec as P

H = 64
P_SIZE = 64
N = 64
G = 4
E = 4096


PRECISE = lax.Precision.HIGHEST
EPSILON = 1e-05


def entering(part, axis, combine, identity, reverse):
    count = lax.axis_size(axis)
    place = lax.axis_index(axis)
    ahead = count - 1 - place if reverse else place
    gathered = jax.tree.map(lambda a: lax.all_gather(a, axis), part)
    state = jax.tree.map(lambda a, e: jnp.zeros_like(a) + jnp.asarray(e, a.dtype), part, identity)

    def one(step, state):
        source = count - 1 - step if reverse else step
        return combine(
            state, jax.tree.map(lambda a: lax.dynamic_index_in_dim(a, source, 0, False), gathered)
        )

    return lax.fori_loop(0, ahead, one, state)


def block_math(state, x_blk, rate_blk, b_blk, c_blk, a_neg):
    block_len = x_blk.shape[0]
    running = jnp.cumsum(rate_blk * a_neg, axis=0)
    log_gap = running[:, None] - running[None, :]
    positions = jnp.arange(block_len)
    causal = (positions[:, None] >= positions[None, :])[:, :, None, None]
    decays = jnp.where(causal, jnp.exp(jnp.where(causal, log_gap, 0.0)), 0.0)
    intersection = jnp.einsum("tgn,sgn->tsg", c_blk, b_blk, precision=PRECISE)
    scores = intersection[..., None] * decays
    scaled = x_blk * rate_blk[..., None]
    within = jnp.einsum("tsgk,sgkp->tgkp", scores, scaled, precision=PRECISE)
    carried = (
        jnp.einsum("tgn,gkpn->tgkp", c_blk, state, precision=PRECISE) * jnp.exp(running)[..., None]
    )
    to_end = jnp.exp(running[-1][None] - running)
    fresh = jnp.einsum("sgkp,sgn->gkpn", scaled * to_end[..., None], b_blk, precision=PRECISE)
    return (state * jnp.exp(running[-1])[..., None, None] + fresh, within + carried)


def local_pass(values, rates, input_matrix_values, c_vals, a_neg):
    tokens_here = values.shape[0]
    heads_group = H // G
    block_len = math.gcd(256, tokens_here)
    block_count = tokens_here // block_len

    def advance(current, pieces):
        return block_math(current, pieces[0], pieces[1], pieces[2], pieces[3], a_neg)

    blocks = (
        values.reshape(block_count, block_len, G, heads_group, P_SIZE),
        rates.reshape(block_count, block_len, G, heads_group),
        input_matrix_values.reshape(block_count, block_len, G, N),
        c_vals.reshape(block_count, block_len, G, N),
    )
    start_state = jnp.zeros((G, heads_group, P_SIZE, N), jnp.float32)
    final_state, within = lax.scan(advance, start_state, blocks)
    running = jnp.cumsum(rates * a_neg, axis=0)
    return (within.reshape(tokens_here, G, heads_group, P_SIZE), running, final_state)


def link_states(earlier, later):
    return (earlier[0] + later[0], jnp.exp(later[0])[:, :, None, None] * earlier[1] + later[1])


def shards(xs, z_gate, b_proj, c_proj, dt_raw, a_log, dt_bias, d_skip, norm_gain, w_out, cotangent):
    tokens_here = xs.shape[1]
    heads_group = H // G
    a_neg = -jnp.exp(a_log).reshape(G, heads_group)
    bias_grid = dt_bias.reshape(G, heads_group)
    skip_grid = d_skip.reshape(G, heads_group)
    values = xs[0].astype(jnp.float32).reshape(tokens_here, G, heads_group, P_SIZE)
    raw_rates = dt_raw[0].astype(jnp.float32).reshape(tokens_here, G, heads_group)
    input_matrix_values = b_proj[0].astype(jnp.float32).reshape(tokens_here, G, N)
    c_vals = c_proj[0].astype(jnp.float32).reshape(tokens_here, G, N)

    def front(values_in, raw_in, b_in, c_in):
        rates = jax.nn.softplus(raw_in + bias_grid)
        return local_pass(values_in, rates, b_in, c_in, a_neg)

    (within, running, final_state), front_back = jax.vjp(
        front, values, raw_rates, input_matrix_values, c_vals
    )

    def finish(within_in, running_in, c_in, values_in, incoming_in):
        carried = (
            jnp.einsum("tgn,gkpn->tgkp", c_in, incoming_in, precision=PRECISE)
            * jnp.exp(running_in)[..., None]
        )
        return (within_in + carried + skip_grid[:, :, None] * values_in).reshape(tokens_here, E)

    running_totals = running[-1]
    start_pair = (jnp.zeros_like(running_totals), jnp.zeros_like(final_state))
    incoming = entering((running_totals, final_state), "ctx", link_states, start_pair, False)[1]
    ssd_out, finish_back = jax.vjp(finish, within, running, c_vals, values, incoming)
    z_float = z_gate[0].astype(jnp.float32)
    z_silu = jax.nn.silu(z_float)
    gated = ssd_out * z_silu
    rscale = lax.rsqrt(jnp.mean(gated * gated, axis=-1, keepdims=True) + EPSILON)
    normed = (gated * rscale * norm_gain).astype(jnp.bfloat16)
    columns = lax.all_to_all(normed, "dp", split_axis=1, concat_axis=0, tiled=True)
    cot_rows = cotangent[0]
    full_weight = lax.all_gather(w_out, "dp", axis=0, tiled=True)
    layer_out = jnp.dot(normed, full_weight, preferred_element_type=jnp.float32).astype(
        jnp.bfloat16
    )
    d_normed = lax.dot_general(
        cot_rows, full_weight, (((1,), (1,)), ((), ())), preferred_element_type=jnp.float32
    ).astype(jnp.bfloat16)
    grad_local = lax.dot_general(
        columns,
        lax.all_gather(cot_rows, "dp", axis=0, tiled=True),
        (((0,), (0,)), ((), ())),
        preferred_element_type=jnp.float32,
    )
    grad_w_out = lax.psum(grad_local, "ctx")
    d_gain_in = d_normed.astype(jnp.float32) * norm_gain
    inner_mean = jnp.mean(d_gain_in * gated, axis=-1, keepdims=True)
    d_gated = rscale * (d_gain_in - gated * rscale * rscale * inner_mean)
    sigma = jax.nn.sigmoid(z_float)
    grad_gate = (d_gated * ssd_out * sigma * (1.0 + z_float * (1.0 - sigma))).astype(jnp.bfloat16)
    d_ssd = d_gated * z_silu
    d_within, d_running, d_c_late, d_values_late, d_incoming = finish_back(d_ssd)
    reach = entering((running_totals, d_incoming), "ctx", link_states, start_pair, True)[1]
    d_totals = jnp.exp(running_totals) * jnp.sum(incoming * reach, axis=(2, 3))
    d_running = d_running.at[-1].add(d_totals)
    d_values, d_raw, d_b, d_c = front_back((d_within, d_running, reach))
    grad_xs = (d_values + d_values_late).reshape(tokens_here, E).astype(jnp.bfloat16)
    grad_b = d_b.reshape(tokens_here, G * N).astype(jnp.bfloat16)
    grad_c = (d_c + d_c_late).reshape(tokens_here, G * N).astype(jnp.bfloat16)
    grad_dt = d_raw.reshape(tokens_here, H).astype(jnp.bfloat16)
    return (
        layer_out[None],
        grad_xs[None],
        grad_gate[None],
        grad_b[None],
        grad_c[None],
        grad_dt[None],
        grad_w_out,
    )


def solution(mesh):
    in_specs = (
        P("dp", "ctx", None),
        P("dp", "ctx", None),
        P("dp", "ctx", None),
        P("dp", "ctx", None),
        P("dp", "ctx", None),
        P(),
        P(),
        P(),
        P(),
        P("dp", None),
        P("dp", "ctx", None),
    )
    out_specs = (
        P("dp", "ctx", None),
        P("dp", "ctx", None),
        P("dp", "ctx", None),
        P("dp", "ctx", None),
        P("dp", "ctx", None),
        P("dp", "ctx", None),
        P("dp", None),
    )
    return jax.shard_map(shards, mesh=mesh, in_specs=in_specs, out_specs=out_specs, check_vma=False)
```

profile of v0, /device:TPU:1, one launch (start us, length us, event | category | flops | bytes accessed | tf_op | source)
XLA Modules:
  0.0 1046.4 jit_solution(11577221745223822978)
XLA Ops:
  15.6 6.9 copy.322
  27.3 124.7 %while.101 = (s32[]{:T(128)}, f32[4,16,64,64]{3,2,1,0:T(8,128)S(1)}, f32[3,64,4,16,64]{4,3,2,1,0:T(8,128)}, f32[3,64,64,4,16]{2,1,4,3,0:T(8,128)}, f32[3,64,64,4...) while((s32[]{:T(128)}, f32[4,16,64,64]{3,2,1,0:T(8,128)S(1)}, ...), condition=%wide.region_2.3_spmd.clone.clone, body=%wide.region_0.2_spmd.clone.clone.sunk | while | flops 622080000 | bytes 41093108 | solution.py:70
  34.8 7.5 fusion.262
  76.4 7.5 fusion.262
  118.0 7.5 fusion.262
  161.9 7.3 copy.331
  172.5 21.7 %all_gather.22 = f32[16,4,16]{2,1,0:T(4,128)S(1)} all-gather(f32[1,4,16]{2,1,0:T(4,128)S(1)} %slice.64), channel_id=1, replica_groups=mesh['dp'=8,'ctx'=16] {'ctx'}, dimensions={0}, use_global_device_ids=true | all-gather | bytes 4352 | tf_op jit(solution)/shard_map/all_gather | solution.py:23
  194.2 133.8 %all-gather.10.cloned.1.call-done = f32[64,16,64,64]{3,2,1,0:T(8,128)} async-done(((f32[4,16,64,64]{3,2,1,0:T(8,128)}), f32[64,16,64,64]{3,2,1,0:T(8,128)}) %all-gather.10.cloned.1.call-update) | async-done | bytes 16777232 | tf_op jit(solution)/shard_map/all_gather | solution.py:23
  330.4 9.1 multiply_reduce_fusion
  345.4 167.6 %all-gather.8.cloned.1.call-done = bf16[4096,2048]{1,0:T(8,128)(2,1)} async-done(((bf16[512,2048]{1,0:T(8,128)(2,1)}), bf16[4096,2048]{1,0:T(8,128)(2,1)}) %all-gather.8.cloned.1.call-update) | async-done | bytes 16777232 | tf_op jit(solution)/shard_map/all_gather | solution.py:116
  513.0 14.5 %multiply_reduce_fusion.1 = (f32[192]{0:T(256)S(1)}, f32[192,4096]{1,0:T(8,128)}) fusion(f32[192,4096]{1,0:T(8,128)} %copy.333, bf16[1,192,4096]{2,1,0:T(8,128)(2,1)S(1)} %copy-done.5, f32[4096]{0:T(1024)S(1)} %copy-done.25, bf16[4096,2048]{1,0:T(8,128)(2,1)} %all-gather.8.cloned.1.call-done, bf16[1,192,2048]{2,1,0:T(8,128)(2,1)} %param.31), kind=kOutput, calls=%fused_computation.196 | convolution fusion | flops 3229875968 | bytes 25445120 | tf_op jit(solution)/shard_map/dot_general | solution.py:120
  580.8 11.5 %fusion.148 = bf16[1,192,2048]{2,1,0:T(8,128)(2,1)} fusion(bf16[4096,2048]{1,0:T(8,128)(2,1)} %all-gather.8.cloned.1.call-done, f32[4096]{0:T(1024)S(1)} %copy-done.25, f32[192]{0:T(256)S(1)} %add_rsqrt_fusion, f32[192,4096]{1,0:T(8,128)} %copy.333, bf16[1,192,4096]{2,1,0:T(8,128)(2,1)S(1)} %copy-done.5), kind=kOutput, calls=%fused_computation.199 | convolution fusion | flops 3228696576 | bytes 22299392 | tf_op jit(solution)/shard_map/dot_general | solution.py:117
  592.4 20.9 %all-gather.14.cloned.1.call-done = bf16[1,1536,2048]{2,1,0:T(8,128)(2,1)} async-done(((bf16[1,192,2048]{2,1,0:T(8,128)(2,1)}), bf16[1,1536,2048]{2,1,0:T(8,128)(2,1)}) %all-gather.14.cloned.1.call-update) | async-done | bytes 6291472 | tf_op jit(solution)/shard_map/all_gather | solution.py:125
  613.3 8.8 fusion.129
  622.1 161.9 %all-gather.12.cloned.1.call-done = f32[64,16,64,64]{3,2,1,0:T(8,128)} async-done(((f32[4,16,64,64]{3,2,1,0:T(8,128)}), f32[64,16,64,64]{3,2,1,0:T(8,128)}) %all-gather.12.cloned.1.call-update) | async-done | bytes 16777232 | tf_op jit(solution)/shard_map/all_gather | solution.py:23
  784.2 28.5 %while.99 = (s32[]{:T(128)}, f32[4,16,64,64]{3,2,1,0:T(8,128)S(1)}, s32[]{:T(128)}, f32[16,4,16]{2,1,0:T(4,128)S(1)}, f32[16,4,16,64,64]{4,3,2,1,0:T(8,128)}, /*index=5*/s32[]{:T(128)}, s32[]{:T(128)}, s32[]{:T(128)}, s32[]{:T(128)}) while((s32[]{:T(128)}, f32[4,16,64,64]{3,2,1,0:T(8,128)S(1)}, s32[]{:T(128)}, f32[16,4,16]{2,1,0:T(4,128)S(1)}, ...), condition=%wide.region_10.11_spmd, body=%wide.region_9.10_spmd.sunk | while | flops 524294 | bytes 3146643 | solution.py:32
  819.8 179.8 %while.100 = (s32[]{:T(128)}, f32[4,16,64,64]{3,2,1,0:T(8,128)}, f32[3,64,4,16,64]{4,3,2,1,0:T(8,128)}, f32[3,64,4,16]{3,2,1,0:T(4,128)}, bf16[3,64,4,64]{3,1,2,...) while((s32[]{:T(128)}, f32[4,16,64,64]{3,2,1,0:T(8,128)}, ...), condition=%wide.region_21.22_spmd.clone.clone, body=%wide.region_11.21_spmd.clone.clone.sunk | while | flops 1239461888 | bytes 50757444 | solution.py:70
  832.8 7.7 fusion.246
  841.6 7.0 fusion.247
  892.8 7.7 fusion.246
  901.5 7.0 fusion.247
  952.5 7.6 fusion.246
  961.1 6.9 fusion.247
  1004.0 10.6 %reduce-window.16 = f32[16,4,2,128]{3,0,1,2:T(8,128)S(1)} reduce-window(f32[16,4,2,128]{3,0,1,2:T(8,128)} %copy.356, f32[]{:T(128)} %constant.242.clone.1), window={size=1x1x1x128 pad=0_0x0_0x0_0x0_127}, to_apply=%region_24.25 | reduce-window | flops 2080768 | bytes 131076 | tf_op jit(solution)/shard_map/reduce-window.2
  (360 shorter events, 391.1 us)
Async XLA Ops:
  7.2 320.9 %all-gather.10.cloned.1.call-start = ((), (), s32[]{:S(2)}) async-start(), calls=%async_computation.3 | async-start | bytes 35651584 | tf_op jit(solution)/shard_map/all_gather | solution.py:23
  8.1 150.8 %copy-start.20 = (f32[4,16]{1,0:T(4,128)}, f32[4,16]{1,0:T(4,128)S(1)}, u32[]{:S(2)}) copy-start(f32[4,16]{1,0:T(4,128)S(1)} %add.153) | copy-start | bytes 772
  15.6 6.9 copy-start.19
  15.6 7.2 copy-start.16
  153.4 359.6 %all-gather.8.cloned.1.call-start = ((), (), s32[]{:S(2)}) async-start(), calls=%async_computation.1 | async-start | bytes 18874368 | tf_op jit(solution)/shard_map/all_gather | solution.py:116
  154.1 459.2 %all-gather.14.cloned.1.call-start = ((), (), s32[]{:S(2)}) async-start(), calls=%async_computation.5 | async-start | bytes 7077888 | tf_op jit(solution)/shard_map/all_gather | solution.py:125
  154.9 629.1 %all-gather.12.cloned.1.call-start = ((), (), s32[]{:S(2)}) async-start(), calls=%async_computation.4 | async-start | bytes 35651584 | tf_op jit(solution)/shard_map/all_gather | solution.py:23
  155.0 6.3 copy-start.13
  161.9 7.4 copy-start.7
  161.9 7.6 copy-start.26
  161.9 7.7 copy-start.4
  330.4 9.1 copy-start.1
  339.5 173.5 %copy-start.5 = (bf16[1,192,4096]{2,1,0:T(8,128)(2,1)S(1)}, bf16[1,192,4096]{2,1,0:T(8,128)(2,1)}, u32[]{:S(2)}) copy-start(bf16[1,192,4096]{2,1,0:T(8,128)(2,1)} %param.22) | copy-start | bytes 4718596
  339.5 173.5 %copy-start.25 = (f32[4096]{0:T(1024)S(1)}, f32[4096]{0:T(1024)}, u32[]{:S(2)}) copy-start(f32[4096]{0:T(1024)} %param.29) | copy-start | bytes 49156
  570.5 42.8 %all-to-all-start = ((bf16[192,8,512]{2,0,1:T(8,128)(2,1)}), bf16[192,8,512]{2,0,1:T(8,128)(2,1)}, u32[]{:S(2)}, u32[]{:S(2)}) async-start(bf16[192,8,512]{2,0,1:T(8,128)(2,1)} %multiply_convert_fusion), calls=%async_computation | async-start | bytes 3145728 | tf_op jit(solution)/shard_map/all_to_all | solution.py:114
  574.8 460.2 %all-reduce.6.cloned.1.call-start = ((), (), s32[]{:S(2)}) async-start(), calls=%async_computation.2 | async-start | bytes 8388608 | tf_op jit(solution)/shard_map/psum | solution.py:129
  999.6 15.1 %copy-start.10 = (f32[3,64,4,16]{3,2,1,0:T(4,128)S(1)}, f32[3,64,4,16]{3,2,1,0:T(4,128)}, u32[]{:S(2)}) copy-start(f32[3,64,4,16]{3,2,1,0:T(4,128)} %get-tuple-element.1041) | copy-start | bytes 147460
  999.6 15.3 %copy-start.11 = (f32[3,64,4,64]{3,1,0,2:T(8,128)S(1)}, f32[3,64,4,64]{3,1,0,2:T(8,128)}, u32[]{:S(2)}) copy-start(f32[3,64,4,64]{3,1,0,2:T(8,128)} %get-tuple-element.1040) | copy-start | bytes 589828
  999.6 15.4 %copy-start.2 = (f32[4,16,64,64]{3,2,1,0:T(8,128)S(1)}, f32[4,16,64,64]{3,2,1,0:T(8,128)}, u32[]{:S(2)}) copy-start(f32[4,16,64,64]{3,2,1,0:T(8,128)} %copy-done.1) | copy-start | bytes 3145732
  1014.7 6.5 copy-start.24
  1021.9 7.8 slice-start
  1021.9 7.9 copy-start.14
  1021.9 7.9 copy-start.21
  1021.9 7.9 copy-start.23
  (10 other events, 33.9 us)
Sparse Core Ops, SparseCore 0:
  153.5 174.5 all-gather.9
  330.4 182.5 all-gather.7
  515.3 97.9 all-gather.13
  614.9 169.0 all-gather.11
  786.9 130.4 all-reduce.5
where the time goes:
time: 1050 us
  waiting for transfers between devices  486 us (46%)
  matrix products  217 us (21%)
  local copies, waits for them, and re-layouts  183 us (17%)
  other arithmetic  118 us (11%)
  blocking collectives  21.7 us (2%)
  between operations  14.6 us (1%)
    all_gather x2, waiting for transfers between devices, entering(): gathered = jax.tree.map(lambda a: lax.all_gather(a, axis), part)  296 us
    all_gather x1, waiting for transfers between devices, shards(): full_weight = lax.all_gather(w_out, 'dp', axis=0, tiled=True)  168 us
    dot_general x9, matrix products, block_math(): within = jnp.einsum('tsgk,sgkp->tgkp', scores, scaled, precision=PRECISE)  66.4 us
    dynamic_update_slice x42, local copies, waits for them, and re-layouts, local_pass(): final_state, within = lax.scan(advance, start_state, blocks)  57.8 us
    dot_general x9, matrix products, block_math(): jnp.einsum('sgkp,sgn->gkpn', scaled * to_end[..., None], b_blk, precision...  46.9 us
    dot_general x9, matrix products, block_math(): jnp.einsum('tgn,gkpn->tgkp', c_blk, state, precision=PRECISE)  38.6 us
    add x15, other arithmetic, link_states(): jnp.exp(later[0])[:, :, None, None] * earlier[1] + later[1]  29.8 us
    dynamic_update_slice x9, other arithmetic, local_pass(): final_state, within = lax.scan(advance, start_state, blocks)  27.3 us
  transfers between devices with their start and end apart: 6, of which 4 were waited for; matrix products, arithmetic and copies ran while one was open for 35% of the time, Pallas kernels for 0%

commit v1 on v0

v1 whole, which is shorter than its diff:
```python
import math

import jax
import jax.numpy as jnp
from jax import lax
from jax.experimental import pallas as pl
from jax.experimental.pallas import tpu as pltpu
from jax.sharding import PartitionSpec as P

H = 64
P_SIZE = 64
N = 64
G = 4
E = 4096
HG = H // G
EG = E // G
EPSILON = 1e-05
LOG2E = math.log2(math.e)
EXT = 80
bf16 = jnp.bfloat16
f32 = jnp.float32
VMEM_LIMIT = 60 * 1024 * 1024


def dot(a, b):
    return lax.dot_general(a, b, (((1,), (0,)), ((), ())), preferred_element_type=f32)


def dot_nt(a, b):
    return lax.dot_general(a, b, (((1,), (1,)), ((), ())), preferred_element_type=f32)


def dot_tn(a, b):
    return lax.dot_general(a, b, (((0,), (0,)), ((), ())), preferred_element_type=f32)


def split3(v):
    a = v.astype(bf16)
    rest = v - a.astype(f32)
    b = rest.astype(bf16)
    c = (rest - b.astype(f32)).astype(bf16)
    return a, b, c


def mask_dot(mask, v):
    a, b, c = split3(v)
    return dot(mask, a) + dot(mask, b) + dot(mask, c)


def low_half(rows):
    return lax.broadcasted_iota(jnp.int32, (rows, 128), 1) < P_SIZE


def pair(values, p, low):
    return jnp.where(low, values[:, 2 * p : 2 * p + 1], values[:, 2 * p + 1 : 2 * p + 2])


def state_kernel(x_ref, b_ref, c_ref, dt_ref, al_ref, bias_ref,
                 s_ref, ext_ref, xr_ref, xw_ref, lg_ref, rg_ref, lt_ref, bg_ref, cg_ref):
    rows = x_ref.shape[0]
    rate = jax.nn.softplus(dt_ref[...].astype(f32) + bias_ref[...])
    steps = rate * (-LOG2E * jnp.exp(al_ref[...]))
    t_pos = lax.broadcasted_iota(jnp.int32, (rows, rows), 0)
    s_pos = lax.broadcasted_iota(jnp.int32, (rows, rows), 1)
    log = mask_dot((t_pos >= s_pos).astype(bf16), steps)
    lt_ref[...] = log.T
    last = log[rows - 1 : rows, :]
    to_end = jnp.exp2(last - log)
    low = low_half(rows)
    low1 = low_half(1)
    for g in range(G):
        lg_ref[g] = log[:, g * HG : (g + 1) * HG]
        rg_ref[g] = rate[:, g * HG : (g + 1) * HG]
        bg_ref[g] = b_ref[:, g * N : (g + 1) * N]
        cg_ref[g] = c_ref[:, g * N : (g + 1) * N]
    for p in range(H // 2):
        lanes = slice(p * 128, (p + 1) * 128)
        xr = x_ref[:, lanes].astype(f32) * pair(rate, p, low)
        xr_ref[:, lanes] = xr.astype(bf16)
        xw_ref[:, lanes] = (xr * pair(to_end, p, low)).astype(bf16)
        total = pair(last, p, low1)
        hi, mid, lo = split3(total)
        ext_ref[N : N + 1, lanes] = hi
        ext_ref[N + 1 : N + 2, lanes] = mid
        ext_ref[N + 2 : N + 3, lanes] = lo
        ext_ref[N + 3 : EXT, lanes] = jnp.zeros((EXT - N - 3, 128), bf16)
    for g in range(G):
        lanes = slice(g * EG, (g + 1) * EG)
        state = dot_tn(bg_ref[g], xw_ref[:, lanes])
        s_ref[:, lanes] = state
        ext_ref[0:N, lanes] = state.astype(bf16)


def link_kernel(reverse, ext_ref, out_ref):
    count = ext_ref.shape[0]
    acc = jnp.zeros((N, ext_ref.shape[2]), f32)
    for step in range(count):
        j = count - 1 - step if reverse else step
        out_ref[j] = acc.astype(bf16)
        rows = ext_ref[j].astype(f32)
        total = rows[N : N + 1] + rows[N + 1 : N + 2] + rows[N + 2 : N + 3]
        acc = jnp.exp2(total) * acc + rows[0:N]


def forward_kernel(x_ref, xr_ref, z_ref, lg_ref, lt_ref, bg_ref, cg_ref, sin_ref, skip_ref, gain_ref,
                   y_ref, normed_ref, r_ref, gated_ref, ss_ref):
    rows = x_ref.shape[0]
    low = low_half(rows)
    low1 = low_half(1)
    t_pos = lax.broadcasted_iota(jnp.int32, (rows, rows), 0)
    s_pos = lax.broadcasted_iota(jnp.int32, (rows, rows), 1)
    causal = t_pos >= s_pos
    ss_ref[...] = jnp.zeros_like(ss_ref)

    def group(g, _):
        base = pl.multiple_of(g * EG, EG)
        log = lg_ref[g]
        log_t = lt_ref[pl.ds(pl.multiple_of(g * HG, HG), HG), :]
        grown = jnp.exp2(log)
        cb = dot_nt(cg_ref[g], bg_ref[g])
        c_blk = cg_ref[g]
        total = ss_ref[...]
        for p in range(HG // 2):
            lanes = pl.ds(pl.multiple_of(base + p * 128, 128), 128)
            parts = []
            for h in (2 * p, 2 * p + 1):
                gap = jnp.where(causal, log[:, h : h + 1] - log_t[h : h + 1, :], -1e30)
                parts.append((cb * jnp.exp2(gap)).astype(bf16))
            both = dot(jnp.concatenate(parts, axis=0), xr_ref[:, lanes])
            y = jnp.where(low, both[:rows], both[rows:])
            y = y + pair(grown, p, low) * dot(c_blk, sin_ref[:, lanes])
            y_ref[:, lanes] = y
            out = y + pair(skip_ref[g], p, low1) * x_ref[:, lanes].astype(f32)
            z = z_ref[:, lanes].astype(f32)
            gated = out * (z * jax.nn.sigmoid(z))
            gated_ref[:, lanes] = gated
            total = total + gated * gated
        ss_ref[...] = total
        return 0

    lax.fori_loop(0, G, group, 0)
    r = lax.rsqrt(jnp.sum(ss_ref[...], axis=1, keepdims=True) * (1.0 / E) + EPSILON)
    r_ref[...] = jnp.broadcast_to(r, r_ref.shape)

    def finish(i, _):
        lanes = pl.ds(pl.multiple_of(i * 512, 512), 512)
        normed_ref[:, lanes] = (gated_ref[:, lanes] * r * gain_ref[:, lanes]).astype(bf16)
        return 0

    lax.fori_loop(0, E // 512, finish, 0)


def gate_kernel(dn_ref, y_ref, x_ref, z_ref, r_ref, lg_ref, cg_ref, skip_ref, gain_ref, ext_ref,
                dz_ref, dy_ref, dyel_ref, gext_ref, acc_ref):
    rows = x_ref.shape[0]
    low = low_half(rows)
    low1 = low_half(1)
    r = r_ref[...]
    acc_ref[...] = jnp.zeros_like(acc_ref)

    def first(g, _):
        base = pl.multiple_of(g * EG, EG)
        acc = acc_ref[...]
        for p in range(HG // 2):
            lanes = pl.ds(pl.multiple_of(base + p * 128, 128), 128)
            z = z_ref[:, lanes].astype(f32)
            out = y_ref[:, lanes] + pair(skip_ref[g], p, low1) * x_ref[:, lanes].astype(f32)
            gated = out * (z * jax.nn.sigmoid(z))
            acc = acc + dn_ref[:, lanes].astype(f32) * gain_ref[:, lanes] * gated
        acc_ref[...] = acc
        return 0

    lax.fori_loop(0, G, first, 0)
    inner = jnp.sum(acc_ref[...], axis=1, keepdims=True) * (1.0 / E)
    scaled = r * r * inner

    def second(g, _):
        base = pl.multiple_of(g * EG, EG)
        grown = jnp.exp2(lg_ref[g])
        for p in range(HG // 2):
            lanes = pl.ds(pl.multiple_of(base + p * 128, 128), 128)
            z = z_ref[:, lanes].astype(f32)
            sig = jax.nn.sigmoid(z)
            silu = z * sig
            out = y_ref[:, lanes] + pair(skip_ref[g], p, low1) * x_ref[:, lanes].astype(f32)
            dg = dn_ref[:, lanes].astype(f32) * gain_ref[:, lanes]
            d_gated = r * (dg - out * silu * scaled)
            dz_ref[:, lanes] = (d_gated * out * (sig * (1.0 + z * (1.0 - sig)))).astype(bf16)
            dy = d_gated * silu
            dy_ref[:, lanes] = dy.astype(bf16)
            dyel_ref[:, lanes] = (dy * pair(grown, p, low)).astype(bf16)
        lanes = pl.ds(base, EG)
        gext_ref[0:N, lanes] = dot_tn(cg_ref[g], dyel_ref[:, lanes]).astype(bf16)
        return 0

    lax.fori_loop(0, G, second, 0)
    gext_ref[N:EXT, :] = ext_ref[N:EXT, :]


def backward_kernel(x_ref, xr_ref, xw_ref, dy_ref, dyel_ref, y_ref, lg_ref, rg_ref, lt_ref, bg_ref, cg_ref,
                    sin_ref, s_ref, reach_ref, skip_ref, dt_ref, al_ref, bias_ref,
                    dx_ref, db_ref, dc_ref, ddt_ref,
                    fresh_ref, q1h_ref, q1l_ref, q2_ref, dcb_ref, qs_ref, dbg_ref, dcg_ref):
    rows = x_ref.shape[0]
    low = low_half(rows)
    low1 = low_half(1)
    s_pos = lax.broadcasted_iota(jnp.int32, (rows, rows), 0)
    t_pos = lax.broadcasted_iota(jnp.int32, (rows, rows), 1)
    causal = t_pos >= s_pos
    e_pos = lax.broadcasted_iota(jnp.int32, (EG, HG), 0)
    h_pos = lax.broadcasted_iota(jnp.int32, (EG, HG), 1)
    heads = ((e_pos // P_SIZE) == h_pos).astype(bf16)

    def group(g, _):
        base = pl.multiple_of(g * EG, EG)
        wide = pl.ds(base, EG)
        log = lg_ref[g]
        rate = rg_ref[g]
        log_t = lt_ref[pl.ds(pl.multiple_of(g * HG, HG), HG), :]
        b_blk = bg_ref[g]
        c_blk = cg_ref[g]
        last = log[rows - 1 : rows, :]
        to_end = jnp.exp2(last - log)
        cbt = dot_nt(b_blk, c_blk)
        reach = reach_ref[:, wide]
        fresh_ref[...] = dot(b_blk, reach)
        dcb_ref[...] = jnp.zeros_like(dcb_ref)
        for p in range(HG // 2):
            here = slice(p * 128, (p + 1) * 128)
            lanes = pl.ds(pl.multiple_of(base + p * 128, 128), 128)
            dy = dy_ref[:, lanes]
            xr = xr_ref[:, lanes]
            decays = []
            parts = []
            for h in (2 * p, 2 * p + 1):
                gap = jnp.where(causal, log_t[h : h + 1, :] - log[:, h : h + 1], -1e30)
                decay = jnp.exp2(gap)
                decays.append(decay)
                parts.append((cbt * decay).astype(bf16))
            both = dot(jnp.concatenate(parts, axis=0), dy)
            dxr = jnp.where(low, both[:rows], both[rows:])
            dxr = dxr + pair(to_end, p, low) * fresh_ref[:, here]
            zero = jnp.zeros_like(xr)
            halves = jnp.concatenate([jnp.where(low, xr, zero), jnp.where(low, zero, xr)], axis=0)
            dm = dot_nt(halves, dy)
            dcb_ref[...] += dm[:rows] * decays[0] + dm[rows:] * decays[1]
            x = x_ref[:, lanes].astype(f32)
            dyf = dy.astype(f32)
            dx_ref[:, lanes] = (dxr * pair(rate, p, low) + pair(skip_ref[g], p, low1) * dyf).astype(bf16)
            q1 = dyf * y_ref[:, lanes] - xr.astype(f32) * dxr
            hi = q1.astype(bf16)
            q1h_ref[:, here] = hi
            q1l_ref[:, here] = (q1 - hi.astype(f32)).astype(bf16)
            q2_ref[:, here] = (x * dxr).astype(bf16)
        dcb = dcb_ref[...].astype(bf16)
        dbg_ref[g] = dot(dcb, c_blk) + dot_nt(xw_ref[:, wide], reach)
        dcg_ref[g] = dot_tn(dcb, b_blk) + dot_nt(dyel_ref[:, wide], sin_ref[:, wide])
        through = (jnp.sum(sin_ref[:, wide].astype(f32) * reach.astype(f32), axis=0, keepdims=True),
                   jnp.sum(s_ref[:, wide] * reach.astype(f32), axis=0, keepdims=True))
        sums = []
        for v in through:
            a, b, _ = split3(jnp.broadcast_to(v, (16, EG)))
            sums.append((dot(a, heads) + dot(b, heads))[0:1])
        at_end = jnp.exp2(last) * sums[0] + sums[1]
        q1 = dot(q1h_ref[...], heads) + dot(q1l_ref[...], heads)
        d_log = mask_dot(causal.astype(bf16), q1) + at_end
        qs_ref[g] = d_log
        rg2 = dot(q2_ref[...], heads)
        qs_ref[G + g] = rg2
        return 0

    lax.fori_loop(0, G, group, 0)
    a_neg = -jnp.exp(al_ref[...])
    slope = jax.nn.sigmoid(dt_ref[...].astype(f32) + bias_ref[...])
    for g in range(G):
        heads_here = slice(g * HG, (g + 1) * HG)
        d_rate = a_neg[:, heads_here] * qs_ref[g] + qs_ref[G + g]
        ddt_ref[:, heads_here] = (d_rate * slope[:, heads_here]).astype(bf16)
        db_ref[:, g * N : (g + 1) * N] = dbg_ref[g].astype(bf16)
        dc_ref[:, g * N : (g + 1) * N] = dcg_ref[g].astype(bf16)


def call(kernel, outs, scratch, *args):
    return pl.pallas_call(
        kernel,
        out_shape=[jax.ShapeDtypeStruct(s, d) for s, d in outs],
        in_specs=[pl.BlockSpec(memory_space=pltpu.VMEM)] * len(args),
        out_specs=[pl.BlockSpec(memory_space=pltpu.VMEM)] * len(outs),
        scratch_shapes=[pltpu.VMEM(s, d) for s, d in scratch],
        compiler_params=pltpu.CompilerParams(vmem_limit_bytes=VMEM_LIMIT),
    )(*args)


def link(ext, reverse):
    count = lax.axis_size("ctx")
    share = E // count
    mine = lax.all_to_all(ext, "ctx", split_axis=1, concat_axis=0, tiled=True).reshape(count, EXT, share)
    (out,) = call(lambda e, o: link_kernel(reverse, e, o), [((count, N, share), bf16)], [], mine)
    return lax.all_to_all(out.reshape(count * N, share), "ctx", split_axis=0, concat_axis=1, tiled=True)


def shards(xs, z_gate, b_proj, c_proj, dt_raw, a_log, dt_bias, d_skip, norm_gain, w_out, cotangent):
    rows = xs.shape[1]
    x, z, b, c, dt, cot = xs[0], z_gate[0], b_proj[0], c_proj[0], dt_raw[0], cotangent[0]
    al, bias, gain = a_log[None], dt_bias[None], norm_gain[None]
    skip = d_skip.reshape(G, 1, HG)
    width = w_out.shape[1]
    full_weight = lax.all_gather(w_out, "dp", axis=0, tiled=True)
    d_normed = lax.dot_general(
        cot, full_weight, (((1,), (1,)), ((), ())), preferred_element_type=f32
    ).astype(bf16)
    wide16 = ((rows, E), bf16)
    s_loc, ext, xr, xw, lg, rg, lt, bg, cg = call(
        state_kernel,
        [((N, E), f32), ((EXT, E), bf16), wide16, wide16, ((G, rows, HG), f32), ((G, rows, HG), f32),
         ((H, rows), f32), ((G, rows, N), bf16), ((G, rows, N), bf16)],
        [], x, b, c, dt, al, bias)
    s_in = link(ext, False)
    y, normed, r = call(
        forward_kernel,
        [((rows, E), f32), wide16, ((rows, 128), f32)],
        [((rows, E), f32), ((rows, 128), f32)],
        x, xr, z, lg, lt, bg, cg, s_in, skip, gain)
    dz, dy, dyel, gext = call(
        gate_kernel,
        [wide16, wide16, wide16, ((EXT, E), bf16)],
        [((rows, 128), f32)],
        d_normed, y, x, z, r, lg, cg, skip, gain, ext)
    reach = link(gext, True)
    dx, db, dc, ddt = call(
        backward_kernel,
        [wide16, ((rows, G * N), bf16), ((rows, G * N), bf16), ((rows, H), bf16)],
        [((rows, EG), f32), ((rows, EG), bf16), ((rows, EG), bf16), ((rows, EG), bf16), ((rows, rows), f32),
         ((2 * G, rows, HG), f32), ((G, rows, N), f32), ((G, rows, N), f32)],
        x, xr, xw, dy, dyel, y, lg, rg, lt, bg, cg, s_in, s_loc, reach, skip, dt, al, bias)

    layer_out = jnp.dot(normed, full_weight, preferred_element_type=f32).astype(bf16)
    columns = lax.all_to_all(normed, "dp", split_axis=1, concat_axis=0, tiled=True)
    cot_all = lax.all_gather(cot, "dp", axis=0, tiled=True)
    grad_local = lax.dot_general(
        columns, cot_all, (((0,), (0,)), ((), ())), preferred_element_type=f32
    ).astype(bf16)
    count = lax.axis_size("ctx")
    pieces = lax.all_to_all(grad_local, "ctx", split_axis=0, concat_axis=0, tiled=True)
    piece = jnp.sum(pieces.reshape(count, -1, width).astype(f32), axis=0).astype(bf16)
    grad_w = lax.all_gather(piece, "ctx", axis=0, tiled=True).astype(f32)
    return layer_out[None], dx[None], dz[None], db[None], dc[None], ddt[None], grad_w


def solution(mesh):
    rows = P("dp", "ctx", None)
    in_specs = (rows,) * 5 + (P(),) * 4 + (P("dp", None), rows)
    out_specs = (rows,) * 6 + (P("dp", None),)
    return jax.shard_map(shards, mesh=mesh, in_specs=in_specs, out_specs=out_specs, check_vma=False)
```

time: 1050 us -> 419 us (0.40)
  waiting for transfers between devices: 486 us -> 193 us
  matrix products: 217 us -> 27.6 us
  local copies, waits for them, and re-layouts: 183 us -> 10.1 us
  other arithmetic: 118 us -> 5.17 us
  blocking collectives: 21.7 us -> 99.7 us
  Pallas kernels: 0 us -> 53.7 us
    all_gather x3 -> x2, waiting for transfers between devices: 317 us -> 16.1 us  [the longest x1 14.3 us: shards(): cot_all = lax.all_gather(cot, 'dp', axis=0, tiled=True)]
    dot_general x42 -> x3, matrix products: 217 us -> 27.6 us  [the longest x1 12.6 us: shards(): lax.dot_general(cot, full_weight, (((1,), (1,)), ((), ())), preferred_ele...]
    all_to_all x0 -> x3, blocking collectives: none -> 99.7 us  [the longest x1 45 us: shards(): lax.all_to_all(normed, 'dp', split_axis=1, concat_axis=0, tiled=True)]
    dynamic_update_slice x42 -> x0, local copies, waits for them, and re-layouts: 57.8 us -> none  [local_pass(): final_state, within = lax.scan(advance, start_state, blocks)]
    pallas_call x0 -> x6, Pallas kernels: none -> 53.7 us  [call(): pl.pallas_call(kernel, out_shape=[jax.ShapeDtypeStruct(s, d) for s, d in...]
    reshape x10 -> x1, local copies, waits for them, and re-layouts: 31.2 us -> 0.66 us  [shards(): skip = d_skip.reshape(G, 1, HG)]
    add x15 -> x0, other arithmetic: 29.8 us -> none  [link_states(): jnp.exp(later[0])[:, :, None, None] * earlier[1] + later[1]]
    dynamic_update_slice x9 -> x0, other arithmetic: 27.3 us -> none  [local_pass(): final_state, within = lax.scan(advance, start_state, blocks)]
  transfers between devices with their start and end apart: 6 -> 6, of which waited for: 4 -> 6; matrix products, arithmetic and copies ran while one was open for 35% -> 9% of each run, Pallas kernels for 0% -> 8%
where the time goes in v1:
time: 419 us; the launch traced here: 418 us
  waiting for transfers between devices  193 us (46%)
  blocking collectives  99.7 us (24%)
  Pallas kernels  53.7 us (13%)
  matrix products  27.6 us (7%)
  starting transfers between devices  15.1 us (4%)
  between operations  13.8 us (3%)
  local copies, waits for them, and re-layouts  10.1 us (2%)
  other arithmetic  5.17 us (1%)
    all_gather x1, waiting for transfers between devices, shards(): full_weight = lax.all_gather(w_out, 'dp', axis=0, tiled=True)  160 us
    pallas_call x6, Pallas kernels, call(): pl.pallas_call(kernel, out_shape=[jax.ShapeDtypeStruct(s, d) for s, d in...  53.7 us
    all_to_all x1, blocking collectives, shards(): lax.all_to_all(normed, 'dp', split_axis=1, concat_axis=0, tiled=True)  45 us
    all_to_all x1, blocking collectives, shards(): lax.all_to_all(grad_local, 'ctx', split_axis=0, concat_axis=0, tiled=True)  36.2 us
    all_to_all x1, blocking collectives, link(): lax.all_to_all(ext, 'ctx', split_axis=1, concat_axis=0, tiled=True)  18.6 us
    all_gather x1, waiting for transfers between devices, shards(): cot_all = lax.all_gather(cot, 'dp', axis=0, tiled=True)  14.3 us
    dot_general x1, matrix products, shards(): lax.dot_general(cot, full_weight, (((1,), (1,)), ((), ())), preferred_ele...  12.6 us
    all_to_all x2, waiting for transfers between devices, link(): lax.all_to_all(out.reshape(count * N, share), 'ctx', split_axis=0, concat...  10 us
  transfers between devices with their start and end apart: 6, of which 6 were waited for; matrix products, arithmetic and copies ran while one was open for 9% of the time, Pallas kernels for 8%

profile of v1, /device:TPU:1, one launch (start us, length us, event | category | flops | bytes accessed | tf_op | source)
XLA Modules:
  0.0 417.8 jit_solution(4178678428579237935)
XLA Ops:
  9.4 8.6 %shard_map.162 = (f32[64,4096]{1,0:T(8,128)}, bf16[80,4096]{1,0:T(8,128)(2,1)}, bf16[192,4096]{1,0:T(8,128)(2,1)}, bf16[192,4096]{1,0:T(8,128)(2,1)}, f32[4,192,...) custom-call(bf16[192,4096]{1,0:T(8,128)(2,1)} %bitcast.54, ...), custom_call_target="tpu_custom_call" | custom-call | tf_op jit(solution)/shard_map/pallas_call | solution.py:284
  19.1 18.6 %all_to_all.92 = bf16[80,16,256]{2,0,1:T(8,128)(2,1)} all-to-all(bf16[80,16,256]{2,0,1:T(8,128)(2,1)S(1)} %bitcast.66), channel_id=1, replica_groups=mesh['dp'=8,'ctx'=16] {'ctx'}, dimensions={1} | all-to-all | bytes 1310720 | tf_op jit(solution)/shard_map/all_to_all | solution.py:297
  37.7 2.0 shard_map.163
  39.7 4.7 %all-to-all-start.1 = ((bf16[16,64,256]{2,1,0:T(8,128)(2,1)}), bf16[16,64,256]{2,1,0:T(8,128)(2,1)S(1)}, u32[]{:S(2)}, u32[]{:S(2)}) async-start(bf16[16,64,256]{2,1,0:T(8,128)(2,1)} %shard_map.163), calls=%async_computation.1 | async-start | bytes 1048576 | tf_op jit(solution)/shard_map/all_to_all | solution.py:299
  45.1 8.9 %all-to-all-done.1 = bf16[16,64,256]{2,1,0:T(8,128)(2,1)S(1)} async-done(((bf16[16,64,256]{2,1,0:T(8,128)(2,1)}), bf16[16,64,256]{2,1,0:T(8,128)(2,1)S(1)}, u32[]{:S(2)}, u32[]{:S(2)}) %all-to-all-start.1) | async-done | bytes 524320 | tf_op jit(solution)/shard_map/all_to_all | solution.py:299
  54.9 10.4 %shard_map.164 = (f32[192,4096]{1,0:T(8,128)}, bf16[192,4096]{1,0:T(8,128)(2,1)}, f32[192,128]{1,0:T(8,128)}) custom-call(bf16[192,4096]{1,0:T(8,128)(2,1)} %bitcast.55, bf16[192,4096]{1,0:T(8,128)(2,1)} %get-tuple-element.27.xr_ref, bf16[192,4096]{1,0:T(8,128)(2,1)} %bitcast.58, f32[4,192,16]{2,1,0:T(8,128)} %get-tuple-element.28.lg_ref, ...), custom_call_target="tpu_custom_call" | custom-call | tf_op jit(solution)/shard_map/pallas_call | solution.py:284
  65.3 1.6 copy.43
  66.8 45.0 %all_to_all.93 = bf16[192,8,512]{2,0,1:T(8,128)(2,1)S(1)} all-to-all(bf16[192,8,512]{2,0,1:T(8,128)(2,1)S(1)} %bitcast.60), channel_id=1, replica_groups=mesh['dp'=8,'ctx'=16] {'dp'}, dimensions={1} | all-to-all | bytes 3145728 | tf_op jit(solution)/shard_map/all_to_all | solution.py:338
  111.8 14.3 %all-gather.9.cloned.1.call-done = bf16[1,1536,2048]{2,1,0:T(8,128)(2,1)} async-done(((bf16[1,192,2048]{2,1,0:T(8,128)(2,1)}), bf16[1,1536,2048]{2,1,0:T(8,128)(2,1)}) %all-gather.9.cloned.1.call-update) | async-done | bytes 6291472 | tf_op jit(solution)/shard_map/all_gather | solution.py:339
  126.1 6.5 %fusion.2 = bf16[512,2048]{1,0:T(8,128)(2,1)S(1)} fusion(bf16[1536,512]{1,0:T(8,128)(2,1)S(1)} %bitcast.72, bf16[1,1536,2048]{2,1,0:T(8,128)(2,1)} %all-gather.9.cloned.1.call-done), kind=kOutput, calls=%fused_computation.3 | convolution fusion | flops 3222274048 | bytes 9961472 | tf_op jit(solution)/shard_map/dot_general | solution.py:340
  132.6 36.2 %all_to_all.94 = bf16[16,32,2048]{2,1,0:T(8,128)(2,1)S(1)} all-to-all(bf16[16,32,2048]{2,1,0:T(8,128)(2,1)S(1)} %bitcast.68), channel_id=1, replica_groups=mesh['dp'=8,'ctx'=16] {'ctx'}, dimensions={0} | all-to-all | bytes 4194304 | tf_op jit(solution)/shard_map/all_to_all | solution.py:344
  169.8 160.3 %all-gather.5.cloned.1.call-done = bf16[4096,2048]{1,0:T(8,128)(2,1)} async-done(((bf16[512,2048]{1,0:T(8,128)(2,1)}), bf16[4096,2048]{1,0:T(8,128)(2,1)}) %all-gather.5.cloned.1.call-update) | async-done | bytes 16777232 | tf_op jit(solution)/shard_map/all_gather | solution.py:308
  330.1 12.6 %convolution_convert_fusion.dn_ref = bf16[192,4096]{1,0:T(8,128)(2,1)} fusion(bf16[4096,2048]{1,0:T(8,128)(2,1)} %all-gather.5.cloned.1.call-done, bf16[1,192,2048]{2,1,0:T(8,128)(2,1)S(1)} %copy-done.2), kind=kOutput, calls=%fused_computation.2 | convolution fusion | flops 3222011904 | bytes 19136512 | tf_op jit(solution)/shard_map/dot_general | solution.py:309
  342.6 12.6 %shard_map.165 = (bf16[192,4096]{1,0:T(8,128)(2,1)}, bf16[192,4096]{1,0:T(8,128)(2,1)}, bf16[192,4096]{1,0:T(8,128)(2,1)}, bf16[80,4096]{1,0:T(8,128)(2,1)}) custom-call(bf16[192,4096]{1,0:T(8,128)(2,1)} %convolution_convert_fusion.dn_ref, f32[192,4096]{1,0:T(8,128)} %get-tuple-element.35.y_ref, bf16[192,4096]{1,0:T(8,128)(2,1)} %bitcast.56, ...), custom_call_target="tpu_custom_call" | custom-call | tf_op jit(solution)/shard_map/pallas_call | solution.py:284
  355.2 2.0 copy.44
  357.2 5.4 %all-to-all-start.2 = ((bf16[80,16,256]{2,0,1:T(8,128)(2,1)}), bf16[80,16,256]{2,0,1:T(8,128)(2,1)S(1)}, u32[]{:S(2)}, u32[]{:S(2)}) async-start(bf16[80,16,256]{2,0,1:T(8,128)(2,1)} %bitcast.52), calls=%async_computation.2 | async-start | bytes 1310720 | tf_op jit(solution)/shard_map/all_to_all | solution.py:297
  362.6 1.8 all-gather.7.cloned.1.call-done
  364.3 4.1 convert_element_type.17
  368.5 4.9 %all-to-all-done.2 = bf16[80,16,256]{2,0,1:T(8,128)(2,1)S(1)} async-done(((bf16[80,16,256]{2,0,1:T(8,128)(2,1)}), bf16[80,16,256]{2,0,1:T(8,128)(2,1)S(1)}, u32[]{:S(2)}, u32[]{:S(2)}) %all-to-all-start.2) | async-done | bytes 655392 | tf_op jit(solution)/shard_map/all_to_all | solution.py:297
  374.2 2.1 shard_map.166
  376.3 4.9 %all-to-all-start.3 = ((bf16[16,64,256]{2,1,0:T(8,128)(2,1)}), bf16[16,64,256]{2,1,0:T(8,128)(2,1)S(1)}, u32[]{:S(2)}, u32[]{:S(2)}) async-start(bf16[16,64,256]{2,1,0:T(8,128)(2,1)} %shard_map.166), calls=%async_computation.3 | async-start | bytes 1048576 | tf_op jit(solution)/shard_map/all_to_all | solution.py:299
  381.2 8.6 %fusion.5 = bf16[1,192,2048]{2,1,0:T(8,128)(2,1)} fusion(bf16[192,4096]{1,0:T(8,128)(2,1)S(1)} %copy-done.1, bf16[4096,2048]{1,0:T(8,128)(2,1)} %all-gather.5.cloned.1.call-done), kind=kOutput, calls=%fused_computation.5 | convolution fusion | flops 3221618688 | bytes 19136512 | tf_op jit(solution)/shard_map/dot_general | solution.py:337
  391.7 18.1 %shard_map.167 = (bf16[192,4096]{1,0:T(8,128)(2,1)}, bf16[192,256]{1,0:T(8,128)(2,1)}, bf16[192,256]{1,0:T(8,128)(2,1)}, bf16[192,64]{1,0:T(8,128)(2,1)}) custom-call(bf16[192,4096]{1,0:T(8,128)(2,1)} %bitcast.57, bf16[192,4096]{1,0:T(8,128)(2,1)} %get-tuple-element.27.xr_ref, bf16[192,4096]{1,0:T(8,128)(2,1)} %get-tuple-element.34.xw_ref, ...), custom_call_target="tpu_custom_call" | custom-call | tf_op jit(solution)/shard_map/pallas_call | solution.py:284
  409.8 1.5 copy.34
  (23 shorter events, 8.7 us)
Async XLA Ops:
  7.2 1.5 copy-start.3
  7.2 118.9 %all-gather.9.cloned.1.call-start = ((), (), s32[]{:S(2)}) async-start(), calls=%async_computation.8 | async-start | bytes 7077888 | tf_op jit(solution)/shard_map/all_gather | solution.py:339
  7.9 322.2 %all-gather.5.cloned.1.call-start = ((), (), s32[]{:S(2)}) async-start(), calls=%async_computation.6 | async-start | bytes 18874368 | tf_op jit(solution)/shard_map/all_gather | solution.py:308
  19.1 25.3 %copy-start.4 = (f32[64]{0:T(128)S(1)}, f32[64]{0:T(128)}, u32[]{:S(2)}) copy-start(f32[64]{0:T(128)} %param.18) | copy-start | bytes 772
  39.7 14.3 %all-to-all-start.1 = ((bf16[16,64,256]{2,1,0:T(8,128)(2,1)}), bf16[16,64,256]{2,1,0:T(8,128)(2,1)S(1)}, u32[]{:S(2)}, u32[]{:S(2)}) async-start(bf16[16,64,256]{2,1,0:T(8,128)(2,1)} %shard_map.163), calls=%async_computation.1 | async-start | bytes 1048576 | tf_op jit(solution)/shard_map/all_to_all | solution.py:299
  44.4 319.9 %all-gather.7.cloned.1.call-start = ((), (), s32[]{:S(2)}) async-start(), calls=%async_computation.7 | async-start | bytes 2228224 | tf_op jit(solution)/shard_map/all_gather | solution.py:346
  168.7 161.3 %copy-start.2 = (bf16[1,192,2048]{2,1,0:T(8,128)(2,1)S(1)}, bf16[1,192,2048]{2,1,0:T(8,128)(2,1)}, u32[]{:S(2)}) copy-start(bf16[1,192,2048]{2,1,0:T(8,128)(2,1)} %param.21) | copy-start | bytes 2359300
  357.2 16.2 %all-to-all-start.2 = ((bf16[80,16,256]{2,0,1:T(8,128)(2,1)}), bf16[80,16,256]{2,0,1:T(8,128)(2,1)S(1)}, u32[]{:S(2)}, u32[]{:S(2)}) async-start(bf16[80,16,256]{2,0,1:T(8,128)(2,1)} %bitcast.52), calls=%async_computation.2 | async-start | bytes 1310720 | tf_op jit(solution)/shard_map/all_to_all | solution.py:297
  368.4 12.7 %copy-start.1 = (bf16[192,4096]{1,0:T(8,128)(2,1)S(1)}, bf16[192,4096]{1,0:T(8,128)(2,1)}, u32[]{:S(2)}) copy-start(bf16[192,4096]{1,0:T(8,128)(2,1)} %get-tuple-element.33) | copy-start | bytes 4718596
  373.4 0.8 copy-start
  376.3 14.6 %all-to-all-start.3 = ((bf16[16,64,256]{2,1,0:T(8,128)(2,1)}), bf16[16,64,256]{2,1,0:T(8,128)(2,1)S(1)}, u32[]{:S(2)}, u32[]{:S(2)}) async-start(bf16[16,64,256]{2,1,0:T(8,128)(2,1)} %shard_map.166), calls=%async_computation.3 | async-start | bytes 1048576 | tf_op jit(solution)/shard_map/all_to_all | solution.py:299
Sparse Core Ops, SparseCore 0:
  10.3 115.7 all-gather.8
  128.5 201.5 all-gather.4
  331.8 32.4 all-gather.6

commit v2 on v1

v2 whole, which is shorter than its diff:
```python
import math

import jax
import jax.numpy as jnp
from jax import lax
from jax.experimental import pallas as pl
from jax.experimental.pallas import tpu as pltpu
from jax.sharding import PartitionSpec as P

H = 64
P_SIZE = 64
N = 64
G = 4
E = 4096
HG = H // G
EG = E // G
EPSILON = 1e-05
LOG2E = math.log2(math.e)
EXT = 80
bf16 = jnp.bfloat16
f32 = jnp.float32
VMEM_LIMIT = 63 * 1024 * 1024
MESH = pl.DeviceIdType.MESH


def dot(a, b):
    return lax.dot_general(a, b, (((1,), (0,)), ((), ())), preferred_element_type=f32)


def dot_nt(a, b):
    return lax.dot_general(a, b, (((1,), (1,)), ((), ())), preferred_element_type=f32)


def dot_tn(a, b):
    return lax.dot_general(a, b, (((0,), (0,)), ((), ())), preferred_element_type=f32)


def split3(v):
    a = v.astype(bf16)
    rest = v - a.astype(f32)
    b = rest.astype(bf16)
    c = (rest - b.astype(f32)).astype(bf16)
    return a, b, c


def mask_dot(mask, v):
    a, b, c = split3(v)
    return dot(mask, a) + dot(mask, b) + dot(mask, c)


def low_half(rows):
    return lax.broadcasted_iota(jnp.int32, (rows, 128), 1) < P_SIZE


def pair(values, p, low):
    return jnp.where(low, values[:, 2 * p : 2 * p + 1], values[:, 2 * p + 1 : 2 * p + 2])


NZ = 4
NX = 4
NDP = 2 * NZ
NCTX = 4 * NX
SHARE = E // NCTX


def layer_kernel(x_ref, z_ref, b_ref, c_ref, dt_ref, al_ref, bias_ref, skip_ref, gain_ref, w_ref, cot_ref,
                 out_ref, dx_ref, dz_ref, db_ref, dc_ref, ddt_ref, gw_ref,
                 w_all, cot_all, nb, nrecv, xr_ref, xw_ref, y_ref, wide_ref, dn_ref, dy_ref, dyel_ref,
                 lay_ref, dcb_ref, qs_ref, dbg_ref, dcg_ref,
                 lg_ref, rg_ref, lt_ref, bg_ref, cg_ref, acc_ref,
                 ext_ref, mine_ref, link_ref, sin_ref, gext_ref, gmine_ref, reach_ref,
                 own_ref, other_ref, sib_ref, rs_ref, piece_ref,
                 local_sem, w_send, w_recv, c_send, c_recv, n_send, n_recv,
                 a_send, a_recv, o_send, o_recv, ga_send, ga_recv, go_send, go_recv,
                 b_send, b_recv, r_send, r_recv, p_send, p_recv, f_send, f_recv):
    rows = x_ref.shape[0]
    width = cot_ref.shape[1]
    half_width = width // 2
    shard = w_ref.shape[0]
    half = shard // 2
    quarter = shard // 4
    dp = lax.axis_index("dp")
    ctx = lax.axis_index("ctx")
    yh, z = dp // NZ, dp % NZ
    x, yl, core = ctx // 4, (ctx // 2) % 2, ctx % 2
    z_up, z_down = (z + 1) % NZ, (z + NZ - 1) % NZ
    z_far = (z + 2) % NZ

    def dev(yh_=yh, z_=z, x_=x, yl_=yl, core_=core):
        return {"dp": yh_ * NZ + z_, "ctx": x_ * 4 + yl_ * 2 + core_}

    up, down = dev(z_=z_up), dev(z_=z_down)
    cross = dev(yh_=1 - yh, yl_=1 - yl)
    sibling = dev(core_=1 - core)

    def remote(src, dst, send, recv, target):
        return pltpu.make_async_remote_copy(
            src_ref=src, dst_ref=dst, send_sem=send, recv_sem=recv, device_id=target, device_id_type=MESH)

    barrier = pltpu.get_barrier_semaphore()

    def greet_ctx(k, _):
        pl.semaphore_signal(barrier, inc=1, device_id={"dp": dp, "ctx": (ctx + k) % NCTX}, device_id_type=MESH)
        return 0

    def greet_plane(k, _):
        pl.semaphore_signal(
            barrier, inc=1, device_id=dev(yh_=(dp + k // 2) % NDP // NZ, z_=(dp + k // 2) % NDP % NZ, yl_=(yl + k) % 2),
            device_id_type=MESH)
        return 0

    lax.fori_loop(1, NCTX, greet_ctx, 0)
    lax.fori_loop(1, 2 * NDP, greet_plane, 0)
    own_w = pltpu.make_async_copy(w_ref, w_all.at[dp], local_sem.at[0])
    own_w.start()
    own_cot = pltpu.make_async_copy(cot_ref, cot_all.at[x], local_sem.at[1])
    own_cot.start()
    pl.semaphore_wait(barrier, NCTX - 1 + 2 * NDP - 1)

    def slot(yh_, z_, start=0, count=half, core_=core):
        return w_all.at[yh_ * NZ + z_, pl.ds(pl.multiple_of(core_ * half + start, quarter), count)]

    def send_w(i, src, dst, target):
        cp = remote(src, dst, w_send.at[i], w_recv.at[i], target)
        cp.start()
        return cp

    mine = w_ref.at[pl.ds(pl.multiple_of(core * half, half), half)]
    w_up = send_w(0, mine, slot(yh, z), up)
    w_down = send_w(1, mine, slot(yh, z), down)
    w_cross = send_w(2, mine, slot(yh, z), cross)
    sent = [w_up, w_down, w_cross]
    shared = {}

    def share(i, yh_, z_):
        cp = send_w(i, slot(yh_, z_), slot(yh_, z_), sibling)
        sent.append(cp)
        return cp

    def send_cot(k):
        return remote(cot_ref, cot_all.at[x], c_send.at[k - 1], c_recv.at[k - 1], dev(x_=(x + k) % NX))

    def send_normed(k):
        return remote(nb.at[(x + k) % NX], nrecv.at[x], n_send.at[k - 1], n_recv.at[k - 1], dev(x_=(x + k) % NX))

    for k in (1, 3, 2):
        send_cot(k).start()

    rate = jax.nn.softplus(dt_ref[...].astype(f32) + bias_ref[...])
    steps = rate * (-LOG2E * jnp.exp(al_ref[...]))
    row_pos = lax.broadcasted_iota(jnp.int32, (rows, rows), 0)
    col_pos = lax.broadcasted_iota(jnp.int32, (rows, rows), 1)
    causal = row_pos >= col_pos
    anticausal = col_pos >= row_pos
    log = mask_dot(causal.astype(bf16), steps)
    lt_ref[...] = log.T
    last = log[rows - 1 : rows, :]
    to_end = jnp.exp2(last - log)
    low = low_half(rows)
    low1 = low_half(1)
    for g in range(G):
        lg_ref[g] = log[:, g * HG : (g + 1) * HG]
        rg_ref[g] = rate[:, g * HG : (g + 1) * HG]
        bg_ref[g] = b_ref[:, g * N : (g + 1) * N]
        cg_ref[g] = c_ref[:, g * N : (g + 1) * N]
    for p in range(H // 2):
        lanes = slice(p * 128, (p + 1) * 128)
        xr = x_ref[:, lanes].astype(f32) * pair(rate, p, low)
        xr_ref[:, lanes] = xr.astype(bf16)
        xw_ref[:, lanes] = (xr * pair(to_end, p, low)).astype(bf16)
        hi, mid, lo = split3(pair(last, p, low1))
        tail = jnp.concatenate([hi, mid, lo, jnp.zeros((EXT - N - 3, 128), bf16)], axis=0)
        ext_ref[N:EXT, lanes] = tail
        gext_ref[N:EXT, lanes] = tail
    for g in range(G):
        lanes = slice(g * EG, (g + 1) * EG)
        state = dot_tn(bg_ref[g], xw_ref[:, lanes])
        ext_ref[0:N, lanes] = state.astype(bf16)

    def lanes_of(j):
        return pl.ds(pl.multiple_of(j * SHARE, SHARE), SHARE)

    def along(k):
        return (ctx + k) % NCTX

    def spread(ext, into, sends, recvs, k):
        return remote(ext.at[:, lanes_of(along(k))], into.at[ctx], sends.at[k - 1], recvs.at[k - 1],
                      {"dp": dp, "ctx": along(k)})

    def back(linked, into, sends, recvs, k):
        return remote(linked.at[along(k)], into.at[:, lanes_of(ctx)], sends.at[k - 1], recvs.at[k - 1],
                      {"dp": dp, "ctx": along(k)})

    def start_all(make):
        lax.fori_loop(1, NCTX, lambda k, _: (make(k).start(), 0)[1], 0)

    def wait_recv_all(make):
        lax.fori_loop(1, NCTX, lambda k, _: (make(k).wait_recv(), 0)[1], 0)

    def wait_send_all(make):
        lax.fori_loop(1, NCTX, lambda k, _: (make(k).wait_send(), 0)[1], 0)

    def link(reverse, gathered, linked, into):
        acc = jnp.zeros((N, SHARE), f32)
        for step in range(NCTX):
            j = NCTX - 1 - step if reverse else step
            linked[j] = acc.astype(bf16)
            part = gathered[j].astype(f32)
            total = part[N : N + 1] + part[N + 1 : N + 2] + part[N + 2 : N + 3]
            acc = jnp.exp2(total) * acc + part[0:N]
        into[:, lanes_of(ctx)] = linked[ctx]

    fwd_out = lambda k: spread(ext_ref, mine_ref, a_send, a_recv, k)
    fwd_back = lambda k: back(link_ref, sin_ref, o_send, o_recv, k)
    rev_out = lambda k: spread(gext_ref, gmine_ref, ga_send, ga_recv, k)
    rev_back = lambda k: back(link_ref, reach_ref, go_send, go_recv, k)
    start_all(fwd_out)
    mine_ref[ctx] = ext_ref[:, lanes_of(ctx)]

    def within(g, _):
        base = pl.multiple_of(g * EG, EG)
        log = lg_ref[g]
        log_t = lt_ref[pl.ds(pl.multiple_of(g * HG, HG), HG), :]
        cb = dot_nt(cg_ref[g], bg_ref[g])
        for p in range(HG // 2):
            lanes = pl.ds(pl.multiple_of(base + p * 128, 128), 128)
            parts = []
            for h in (2 * p, 2 * p + 1):
                gap = jnp.where(causal, log[:, h : h + 1] - log_t[h : h + 1, :], -1e30)
                parts.append((cb * jnp.exp2(gap)).astype(bf16))
            both = dot(jnp.concatenate(parts, axis=0), xr_ref[:, lanes])
            y_ref[:, lanes] = jnp.where(low, both[:rows], both[rows:])
        return 0

    lax.fori_loop(0, G, within, 0)
    wait_recv_all(fwd_out)
    link(False, mine_ref, link_ref, sin_ref)
    start_all(fwd_back)

    w_up.wait_recv()
    sent.append(send_w(3, slot(yh, z_down, 0, quarter), slot(yh, z_down, 0, quarter), up))
    w_down.wait_recv()
    sent.append(send_w(4, slot(yh, z_up, quarter, quarter), slot(yh, z_up, quarter, quarter), down))
    w_cross.wait_recv()
    sent.append(send_w(5, slot(1 - yh, z), slot(1 - yh, z), up))
    sent.append(send_w(6, slot(1 - yh, z), slot(1 - yh, z), down))
    w_far1, w_far2, w_cup, w_cdown = sent[3:7]
    shared[0] = share(8, yh, z_down)
    shared[1] = share(9, yh, z_up)
    shared[2] = share(10, 1 - yh, z)

    wait_recv_all(fwd_back)

    acc_ref[...] = jnp.zeros_like(acc_ref)

    def gate(g, _):
        base = pl.multiple_of(g * EG, EG)
        grown = jnp.exp2(lg_ref[g])
        c_blk = cg_ref[g]
        total = acc_ref[...]
        for p in range(HG // 2):
            lanes = pl.ds(pl.multiple_of(base + p * 128, 128), 128)
            y = y_ref[:, lanes] + pair(grown, p, low) * dot(c_blk, sin_ref[:, lanes])
            y_ref[:, lanes] = y
            out = y + pair(skip_ref[g], p, low1) * x_ref[:, lanes].astype(f32)
            zf = z_ref[:, lanes].astype(f32)
            gated = out * (zf * jax.nn.sigmoid(zf))
            wide_ref[:, lanes] = gated
            total = total + gated * gated
        acc_ref[...] = total
        return 0

    lax.fori_loop(0, G, gate, 0)
    r = lax.rsqrt(jnp.sum(acc_ref[...], axis=1, keepdims=True) * (1.0 / E) + EPSILON)

    def norm(i, _):
        for q in range(NX):
            lanes = pl.ds(pl.multiple_of(i * 512 + q * 128, 128), 128)
            nb[q, :, pl.ds(pl.multiple_of(i * 128, 128), 128)] = (
                wide_ref[:, lanes] * r * gain_ref[:, lanes]).astype(bf16)
        return 0

    lax.fori_loop(0, NDP, norm, 0)
    for k in (1, 3, 2):
        send_normed(k).start()
    nrecv[x] = nb[x]

    own_w.wait()
    own_cot.wait()
    lay_ref[...] = jnp.zeros_like(lay_ref)

    def project(yh_, z_):
        k = yh_ * NZ + z_
        dn_ref[:, pl.ds(pl.multiple_of(k * shard, shard), shard)] = dot_nt(cot_all[x], w_all[k]).astype(bf16)
        block = jnp.concatenate([nb[q, :, pl.ds(pl.multiple_of(k * 128, 128), 128)] for q in range(NX)], axis=1)

        def tile(n, _):
            cols = pl.ds(pl.multiple_of(n * (width // 4), width // 4), width // 4)
            lay_ref[:, cols] += dot(block, w_all[k, :, cols])
            return 0

        lax.fori_loop(0, 4, tile, 0)

    project(yh, z)
    shared[0].wait_recv()
    project(yh, z_down)
    shared[1].wait_recv()
    project(yh, z_up)
    shared[2].wait_recv()
    project(1 - yh, z)
    w_far1.wait_recv()
    w_far2.wait_recv()
    w_last = send_w(7, slot(yh, z_far), slot(yh, z_far), cross)
    sent.append(w_last)
    shared[3] = share(11, yh, z_far)
    w_cup.wait_recv()
    shared[4] = share(12, 1 - yh, z_down)
    w_cdown.wait_recv()
    shared[5] = share(13, 1 - yh, z_up)
    shared[3].wait_recv()
    project(yh, z_far)
    shared[4].wait_recv()
    project(1 - yh, z_down)
    shared[5].wait_recv()
    project(1 - yh, z_up)

    for k in (1, 3, 2):
        send_cot(k).wait_recv()
        send_normed(k).wait_recv()

    def block_of(k):
        return (dp + k) % NDP

    def send_half(k):
        i = block_of(k)
        return remote(other_ref.at[i], sib_ref.at[i], b_send.at[k], b_recv.at[k], sibling)

    def weigh(k, _):
        i = block_of(k)
        lanes = pl.ds(pl.multiple_of(i * 128, 128), 128)

        def product(side):
            cols = pl.ds(pl.multiple_of(side * half_width, half_width), half_width)
            total = dot_tn(nrecv[0, :, lanes], cot_all[0, :, cols])
            for s in range(1, NX):
                total = total + dot_tn(nrecv[s, :, lanes], cot_all[s, :, cols])
            return total.astype(bf16)

        other_ref[i] = product(1 - core)
        send_half(k).start()
        own_ref[i] = product(core)
        return 0

    lax.fori_loop(0, NDP, weigh, 0)

    def send_piece(k, j):
        i = block_of(k)
        other = (yl + j) % 2
        return remote(own_ref.at[i, pl.ds(pl.multiple_of(other * 64, 64), 64)], rs_ref.at[dp * 2 + yl],
                      r_send.at[2 * k + j], r_recv.at[2 * k + j], dev(yh_=i // NZ, z_=i % NZ, yl_=other))

    def combine(k, _):
        i = block_of(k)
        send_half(k).wait_recv()
        own_ref[i] = (own_ref[i].astype(f32) + sib_ref[i].astype(f32)).astype(bf16)
        return 0

    def send_both(k, _):
        combine(k, 0)
        send_piece(k, 0).start()
        send_piece(k, 1).start()
        return 0

    combine(0, 0)
    send_piece(0, 1).start()
    lax.fori_loop(1, NDP, send_both, 0)
    rs_ref[dp * 2 + yl] = own_ref[dp, pl.ds(pl.multiple_of(yl * 64, 64), 64)]

    w_last.wait_recv()
    shared[6] = share(14, 1 - yh, z_far)
    shared[6].wait_recv()
    project(1 - yh, z_far)
    out_ref[...] = lay_ref[...].astype(bf16)

    acc_ref[...] = jnp.zeros_like(acc_ref)

    def mean(g, _):
        base = pl.multiple_of(g * EG, EG)
        acc = acc_ref[...]
        for p in range(HG // 2):
            lanes = pl.ds(pl.multiple_of(base + p * 128, 128), 128)
            acc = acc + dn_ref[:, lanes].astype(f32) * gain_ref[:, lanes] * wide_ref[:, lanes]
        acc_ref[...] = acc
        return 0

    lax.fori_loop(0, G, mean, 0)
    inner = jnp.sum(acc_ref[...], axis=1, keepdims=True) * (1.0 / E)
    scaled = r * r * inner

    def gate_back(g, _):
        base = pl.multiple_of(g * EG, EG)
        grown = jnp.exp2(lg_ref[g])
        for p in range(HG // 2):
            lanes = pl.ds(pl.multiple_of(base + p * 128, 128), 128)
            zf = z_ref[:, lanes].astype(f32)
            sig = jax.nn.sigmoid(zf)
            silu = zf * sig
            out = y_ref[:, lanes] + pair(skip_ref[g], p, low1) * x_ref[:, lanes].astype(f32)
            dg = dn_ref[:, lanes].astype(f32) * gain_ref[:, lanes]
            d_gated = r * (dg - wide_ref[:, lanes] * scaled)
            dz_ref[:, lanes] = (d_gated * out * (sig * (1.0 + zf * (1.0 - sig)))).astype(bf16)
            dy = d_gated * silu
            dy_ref[:, lanes] = dy.astype(bf16)
            dyel_ref[:, lanes] = (dy * pair(grown, p, low)).astype(bf16)
        lanes = pl.ds(base, EG)
        gext_ref[0:N, lanes] = dot_tn(cg_ref[g], dyel_ref[:, lanes]).astype(bf16)
        return 0

    lax.fori_loop(0, G, gate_back, 0)
    start_all(rev_out)
    gmine_ref[ctx] = gext_ref[:, lanes_of(ctx)]

    def within_back(g, _):
        base = pl.multiple_of(g * EG, EG)
        log = lg_ref[g]
        log_t = lt_ref[pl.ds(pl.multiple_of(g * HG, HG), HG), :]
        cbt = dot_nt(bg_ref[g], cg_ref[g])
        for p in range(HG // 2):
            lanes = pl.ds(pl.multiple_of(base + p * 128, 128), 128)
            dy = dy_ref[:, lanes]
            xr = xr_ref[:, lanes]
            decays = []
            parts = []
            for h in (2 * p, 2 * p + 1):
                gap = jnp.where(anticausal, log_t[h : h + 1, :] - log[:, h : h + 1], -1e30)
                decay = jnp.exp2(gap)
                decays.append(decay)
                parts.append((cbt * decay).astype(bf16))
            both = dot(jnp.concatenate(parts, axis=0), dy)
            wide_ref[:, lanes] = jnp.where(low, both[:rows], both[rows:])
            zero = jnp.zeros_like(xr)
            halves = jnp.concatenate([jnp.where(low, xr, zero), jnp.where(low, zero, xr)], axis=0)
            dm = dot_nt(halves, dy)
            add = dm[:rows] * decays[0] + dm[rows:] * decays[1]
            if p == 0:
                dcb_ref[g] = add
            else:
                dcb_ref[g] += add
        return 0

    lax.fori_loop(0, G // 2, within_back, 0)
    wait_recv_all(rev_out)
    wait_send_all(fwd_back)
    link(True, gmine_ref, link_ref, reach_ref)
    start_all(rev_back)
    lax.fori_loop(G // 2, G, within_back, 0)

    for k in range(NDP):
        for j in range(2):
            if k + j > 0:
                send_piece(k, j).wait_recv()

    total = rs_ref[0].astype(f32)
    for q in range(1, 2 * NDP):
        total = total + rs_ref[q].astype(f32)
    piece_ref[...] = total.astype(bf16)

    def ring(k):
        return (x + k // 2) % NX, (yl + k) % 2

    def ring_from(k):
        return (x + NX - k // 2) % NX * 4 + (yl + k) % 2 * 2 + core

    def send_sum(k):
        x_, yl_ = ring(k)
        return remote(piece_ref, gw_ref.at[ctx], p_send.at[k], p_recv.at[k], dev(x_=x_, yl_=yl_))

    def hand_on(k):
        src = gw_ref.at[ring_from(k)]
        return remote(src, src, f_send.at[k], f_recv.at[k], sibling)

    for k in range(1, 2 * NX):
        send_sum(k).start()
    to_sibling = remote(piece_ref, gw_ref.at[ctx], p_send.at[0], p_recv.at[0], sibling)
    to_sibling.start()
    own_piece = pltpu.make_async_copy(piece_ref, gw_ref.at[ctx], local_sem.at[2])
    own_piece.start()

    wait_recv_all(rev_back)

    e_pos = lax.broadcasted_iota(jnp.int32, (EG, HG), 0)
    h_pos = lax.broadcasted_iota(jnp.int32, (EG, HG), 1)
    heads = ((e_pos // P_SIZE) == h_pos).astype(bf16)

    def finish(g, _):
        base = pl.multiple_of(g * EG, EG)
        wide = pl.ds(base, EG)
        log = lg_ref[g]
        rate = rg_ref[g]
        b_blk = bg_ref[g]
        c_blk = cg_ref[g]
        last = log[rows - 1 : rows, :]
        to_end = jnp.exp2(last - log)
        for p in range(HG // 2):
            here = slice(p * 128, (p + 1) * 128)
            lanes = pl.ds(pl.multiple_of(base + p * 128, 128), 128)
            dyf = dy_ref[:, lanes].astype(f32)
            dxr = wide_ref[:, lanes] + pair(to_end, p, low) * dot(b_blk, reach_ref[:, lanes])
            dy_ref[:, lanes] = (dxr * pair(rate, p, low) + pair(skip_ref[g], p, low1) * dyf).astype(bf16)
            q1 = dyf * y_ref[:, lanes] - xr_ref[:, lanes].astype(f32) * dxr
            hi = q1.astype(bf16)
            dn_ref[:, here] = hi
            dn_ref[:, slice(EG + p * 128, EG + (p + 1) * 128)] = (q1 - hi.astype(f32)).astype(bf16)
            dn_ref[:, slice(2 * EG + p * 128, 2 * EG + (p + 1) * 128)] = (x_ref[:, lanes].astype(f32) * dxr).astype(bf16)
        reach = reach_ref[:, wide]
        dcb = dcb_ref[g].astype(bf16)
        dbg_ref[g] = (dot(dcb, c_blk) + dot_nt(xw_ref[:, wide], reach)).astype(bf16)
        dcg_ref[g] = (dot_tn(dcb, b_blk) + dot_nt(dyel_ref[:, wide], sin_ref[:, wide])).astype(bf16)
        sums = []
        for v in (sin_ref[:, wide].astype(f32), ext_ref[0:N, wide].astype(f32)):
            v = jnp.sum(v * reach.astype(f32), axis=0, keepdims=True)
            a, b, _ = split3(jnp.broadcast_to(v, (16, EG)))
            sums.append((dot(a, heads) + dot(b, heads))[0:1])
        at_end = jnp.exp2(last) * sums[0] + sums[1]
        q1 = dot(dn_ref[:, 0:EG], heads) + dot(dn_ref[:, EG : 2 * EG], heads)
        qs_ref[g] = mask_dot(anticausal.astype(bf16), q1) + at_end
        qs_ref[G + g] = dot(dn_ref[:, 2 * EG : 3 * EG], heads)
        return 0

    lax.fori_loop(0, G, finish, 0)
    dx_out = pltpu.make_async_copy(dy_ref, dx_ref, local_sem.at[3])
    dx_out.start()
    a_neg = -jnp.exp(al_ref[...])
    slope = jax.nn.sigmoid(dt_ref[...].astype(f32) + bias_ref[...])
    for g in range(G):
        here = slice(g * HG, (g + 1) * HG)
        d_rate = a_neg[:, here] * qs_ref[g] + qs_ref[G + g]
        ddt_ref[:, here] = (d_rate * slope[:, here]).astype(bf16)
        db_ref[:, g * N : (g + 1) * N] = dbg_ref[g]
        dc_ref[:, g * N : (g + 1) * N] = dcg_ref[g]

    for k in range(1, 2 * NX):
        send_sum(k).wait_recv()
        hand_on(k).start()

    dx_out.wait()
    own_piece.wait()
    to_sibling.wait()
    for k in range(1, 2 * NX):
        send_sum(k).wait_send()
        hand_on(k).wait()
    for cp in sent:
        cp.wait_send()
    for k in (1, 3, 2):
        send_cot(k).wait_send()
        send_normed(k).wait_send()
    for make in (fwd_out, rev_out, rev_back):
        wait_send_all(make)
    for k in range(NDP):
        send_half(k).wait_send()
        for j in range(2):
            if k + j > 0:
                send_piece(k, j).wait_send()


def shards(xs, z_gate, b_proj, c_proj, dt_raw, a_log, dt_bias, d_skip, norm_gain, w_out, cotangent):
    rows = xs.shape[1]
    width = cotangent.shape[2]
    shard = w_out.shape[0]
    wide = ((rows, E), bf16)
    outs = [((rows, width), bf16), wide, wide, ((rows, G * N), bf16), ((rows, G * N), bf16), ((rows, H), bf16),
            ((NCTX, shard // 8, width // 2), bf16)]
    state = ((N, E), bf16)
    ext = ((EXT, E), bf16)
    share = ((NCTX, EXT, SHARE), bf16)
    linked = ((NCTX, N, SHARE), bf16)
    per_group = ((G, rows, HG), f32)
    group_cols = ((G, rows, N), bf16)
    quad = ((NX, rows, E // NX), bf16)
    block = ((NDP, 128, width // 2), bf16)
    scratch = [
        ((NDP, shard, width), bf16), ((NX, rows, width), bf16), quad, quad, wide, wide, ((rows, E), f32),
        ((rows, E), f32), wide, wide, wide,
        ((rows, width), f32), ((G, rows, rows), f32),
        ((2 * G, rows, HG), f32), group_cols, group_cols,
        per_group, per_group, ((H, rows), f32), group_cols, group_cols, ((rows, 128), f32),
        ext, share, linked, state, ext, share, state,
        block, block, block, ((2 * NDP, 64, width // 2), bf16), ((64, width // 2), bf16),
    ]
    sems = [4, 15, 15, 3, 3, 3, 3] + [NCTX - 1] * 8 + [NDP, NDP, 2 * NDP, 2 * NDP] + [2 * NX] * 4
    vmem = pl.BlockSpec(memory_space=pltpu.VMEM)
    hbm = pl.BlockSpec(memory_space=pl.ANY)
    layer_out, dx, dz, db, dc, ddt, gw = pl.pallas_call(
        layer_kernel,
        out_shape=[jax.ShapeDtypeStruct(s, d) for s, d in outs],
        in_specs=[vmem] * 9 + [hbm, hbm],
        out_specs=[vmem, hbm] + [vmem] * 4 + [hbm],
        scratch_shapes=[pltpu.VMEM(s, d) for s, d in scratch] + [pltpu.SemaphoreType.DMA((n,)) for n in sems],
        compiler_params=pltpu.CompilerParams(
            collective_id=0, has_side_effects=True, vmem_limit_bytes=VMEM_LIMIT),
    )(xs[0], z_gate[0], b_proj[0], c_proj[0], dt_raw[0], a_log[None], dt_bias[None],
      d_skip.reshape(G, 1, HG), norm_gain[None], w_out, cotangent[0])
    gw = gw.reshape(NX, 2, 2, 64, width // 2).transpose(0, 1, 3, 2, 4).reshape(shard, width).astype(f32)
    return layer_out[None], dx[None], dz[None], db[None], dc[None], ddt[None], gw


def solution(mesh):
    rows = P("dp", "ctx", None)
    in_specs = (rows,) * 5 + (P(),) * 4 + (P("dp", None), rows)
    out_specs = (rows,) * 6 + (P("dp", None),)
    return jax.shard_map(shards, mesh=mesh, in_specs=in_specs, out_specs=out_specs, check_vma=False)
```

time: 419 us -> 188 us (0.45)
  waiting for transfers between devices: 193 us -> 0 us
  Pallas kernels: 53.7 us -> 167 us
  blocking collectives: 99.7 us -> 0 us
  matrix products: 27.6 us -> 0 us
  starting transfers between devices: 15.1 us -> 0 us
  between operations: 13.8 us -> 0.67 us
  local copies, waits for them, and re-layouts: 10.1 us -> 16.8 us
    all_gather x3 -> x0, waiting for transfers between devices: 176 us -> none  [the longest x1 160 us: shards(): full_weight = lax.all_gather(w_out, 'dp', axis=0, tiled=True)]
    pallas_call x6 -> x1, Pallas kernels: 53.7 us -> 167 us  [shards(): pl.pallas_call(layer_kernel, out_shape=[jax.ShapeDtypeStruct(s, d) for s,...]
    all_to_all x3 -> x0, blocking collectives: 99.7 us -> none  [the longest x1 45 us: shards(): lax.all_to_all(normed, 'dp', split_axis=1, concat_axis=0, tiled=True)]
    dot_general x3 -> x0, matrix products: 27.6 us -> none  [the longest x1 12.6 us: shards(): lax.dot_general(cot, full_weight, (((1,), (1,)), ((), ())), preferred_ele...]
    all_to_all x3 -> x0, waiting for transfers between devices: 15 us -> none  [the longest x2 10 us: link(): lax.all_to_all(out.reshape(count * N, share), 'ctx', split_axis=0, concat...]
    all_to_all x3 -> x0, starting transfers between devices: 14.9 us -> none  [the longest x2 9.58 us: link(): lax.all_to_all(out.reshape(count * N, share), 'ctx', split_axis=0, concat...]
    unnamed x12 -> x18, local copies, waits for them, and re-layouts: 3.08 us -> 12.2 us
    all_to_all x5 -> x0, local copies, waits for them, and re-layouts: 6.36 us -> none  [the longest x2 3.11 us: link(): lax.all_to_all(ext, 'ctx', split_axis=1, concat_axis=0, tiled=True)]
  transfers between devices with their start and end apart: 6 -> 0, of which waited for: 6 -> 0; matrix products, arithmetic and copies ran while one was open for 9% -> 0% of each run, Pallas kernels for 8% -> 0%
where the time goes in v2:
time: 188 us; the launch traced here: 186 us
  Pallas kernels  167 us (89%)
  local copies, waits for them, and re-layouts  16.8 us (9%)
  other arithmetic  2.05 us (1%)
    pallas_call x1, Pallas kernels, shards(): pl.pallas_call(layer_kernel, out_shape=[jax.ShapeDtypeStruct(s, d) for s,...  167 us
    unnamed x18, local copies, waits for them, and re-layouts  12.2 us

profile of v2, /device:TPU:1, one launch (start us, length us, event | category | flops | bytes accessed | tf_op | source)
XLA Modules:
  0.0 186.3 jit_solution(10926983370583097508)
XLA Ops:
  0.6 1.3 reshape.23
  1.9 1.5 copy.18
  3.4 166.8 %shard_map.162 = (bf16[192,2048]{1,0:T(8,128)(2,1)}, bf16[192,4096]{1,0:T(8,128)(2,1)}, bf16[192,4096]{1,0:T(8,128)(2,1)}, bf16[192,256]{1,0:T(8,128)(2,1)}, bf1...) custom-call(bf16[192,4096]{1,0:T(8,128)(2,1)} %bitcast.28, ...), custom_call_target="tpu_custom_call" | custom-call | tf_op jit(solution)/shard_map/pallas_call | solution.py:593
  170.2 1.5 copy.21
  171.7 2.1 %convert_bitcast_fusion = f32[4,2,64,2,1024]{4,2,3,1,0:T(8,128)S(1)} fusion(bf16[4,2,2,64,1024]{4,3,2,1,0:T(8,128)(2,1)} %bitcast.25), kind=kLoop, calls=%fused_computation | loop fusion | flops 1048576 | bytes 6291456 | tf_op jit(solution)/shard_map/convert_element_type | solution.py:603
  173.8 3.2 %copy.20 = f32[4,2,64,2,1024]{4,3,2,1,0:T(2,128)S(1)} copy(f32[4,2,64,2,1024]{4,2,3,1,0:T(8,128)S(1)} %convert_bitcast_fusion) | data formatting | bytes 8388608 | tf_op jit(solution)/shard_map/convert_element_type | solution.py:603
  177.0 0.0 copy-start.2
  177.0 4.0 %copy.22 = f32[64,8,2,1024]{3,1,2,0:T(8,128)} copy(f32[64,8,2,1024]{3,2,1,0:T(2,128)S(1)} %bitcast.23) | data formatting | bytes 8388608
  181.0 0.0 copy-start.1
  181.0 0.0 copy-done.2
  181.0 0.0 copy-start
  181.0 0.9 copy.28
  181.9 0.8 copy-done.1
  182.7 1.1 copy.29
  183.8 0.0 copy-done
  183.8 0.0 copy-start.4
  183.8 0.0 copy-start.3
  183.8 1.1 copy.30
  185.0 0.0 copy-done.4
  185.0 0.6 copy.31
  185.6 0.0 copy-done.3
  185.6 0.6 copy.32
Async XLA Ops:
  177.0 4.0 %copy-start.2 = (bf16[192,2048]{1,0:T(8,128)(2,1)S(1)}, bf16[192,2048]{1,0:T(8,128)(2,1)}, u32[]{:S(2)}) copy-start(bf16[192,2048]{1,0:T(8,128)(2,1)} %get-tuple-element.14) | copy-start | bytes 2359300
  181.0 1.7 copy-start.1
  181.0 2.8 %copy-start = (bf16[192,4096]{1,0:T(8,128)(2,1)S(1)}, bf16[192,4096]{1,0:T(8,128)(2,1)}, u32[]{:S(2)}) copy-start(bf16[192,4096]{1,0:T(8,128)(2,1)} %get-tuple-element.16) | copy-start | bytes 4718596
  183.8 1.1 copy-start.4
  183.8 1.8 copy-start.3

commit v3 on v2

--- a/solution.py
+++ b/solution.py
@@ -63,13 +63,13 @@
 SHARE = E // NCTX
 
 
-def layer_kernel(x_ref, z_ref, b_ref, c_ref, dt_ref, al_ref, bias_ref, skip_ref, gain_ref, w_ref, cot_ref,
-                 out_ref, dx_ref, dz_ref, db_ref, dc_ref, ddt_ref, gw_ref,
-                 w_all, cot_all, nb, nrecv, xr_ref, xw_ref, y_ref, wide_ref, dn_ref, dy_ref, dyel_ref,
+def layer_kernel(x_in, z_in, b_ref, c_ref, dt_ref, al_ref, bias_ref, skips_ref, gain_ref, w_ref, cot_ref,
+                 layer_ref, dx_ref, dz_out, db_ref, dc_ref, ddt_ref, gw_ref,
+                 x_ref, z_ref, out_ref, dz_ref, w_all, cot_all, nb, nrecv, xr_ref, xw_ref, y_ref, wide_ref, dn_ref, dy_ref, dyel_ref,
                  lay_ref, dcb_ref, qs_ref, dbg_ref, dcg_ref,
-                 lg_ref, rg_ref, lt_ref, bg_ref, cg_ref, acc_ref,
+                 lg_ref, rg_ref, lt_ref, bg_ref, cg_ref, acc_ref, skip_ref,
                  ext_ref, mine_ref, link_ref, sin_ref, gext_ref, gmine_ref, reach_ref,
-                 own_ref, other_ref, sib_ref, rs_ref, piece_ref,
+                 own_ref, other_ref, sib_ref, ra1_ref, rb1_ref, ra2_ref, rb2_ref, piece_ref,
                  local_sem, w_send, w_recv, c_send, c_recv, n_send, n_recv,
                  a_send, a_recv, o_send, o_recv, ga_send, ga_recv, go_send, go_recv,
                  b_send, b_recv, r_send, r_recv, p_send, p_recv, f_send, f_recv):
@@ -97,56 +97,21 @@
         return pltpu.make_async_remote_copy(
             src_ref=src, dst_ref=dst, send_sem=send, recv_sem=recv, device_id=target, device_id_type=MESH)
 
+    x_copy = pltpu.make_async_copy(x_in, x_ref, local_sem.at[4])
+    x_copy.start()
+    z_copy = pltpu.make_async_copy(z_in, z_ref, local_sem.at[5])
+    z_copy.start()
+
     barrier = pltpu.get_barrier_semaphore()
 
     def greet_ctx(k, _):
         pl.semaphore_signal(barrier, inc=1, device_id={"dp": dp, "ctx": (ctx + k) % NCTX}, device_id_type=MESH)
         return 0
 
-    def greet_plane(k, _):
-        pl.semaphore_signal(
-            barrier, inc=1, device_id=dev(yh_=(dp + k // 2) % NDP // NZ, z_=(dp + k // 2) % NDP % NZ, yl_=(yl + k) % 2),
-            device_id_type=MESH)
-        return 0
-
+    for other in [dev(z_=(z + k) % NZ) for k in (1, 2, 3)] + [dev(yh_=1 - yh, yl_=k) for k in (0, 1)]:
+        pl.semaphore_signal(barrier, inc=1, device_id=other, device_id_type=MESH)
     lax.fori_loop(1, NCTX, greet_ctx, 0)
-    lax.fori_loop(1, 2 * NDP, greet_plane, 0)
-    own_w = pltpu.make_async_copy(w_ref, w_all.at[dp], local_sem.at[0])
-    own_w.start()
-    own_cot = pltpu.make_async_copy(cot_ref, cot_all.at[x], local_sem.at[1])
-    own_cot.start()
-    pl.semaphore_wait(barrier, NCTX - 1 + 2 * NDP - 1)
-
-    def slot(yh_, z_, start=0, count=half, core_=core):
-        return w_all.at[yh_ * NZ + z_, pl.ds(pl.multiple_of(core_ * half + start, quarter), count)]
-
-    def send_w(i, src, dst, target):
-        cp = remote(src, dst, w_send.at[i], w_recv.at[i], target)
-        cp.start()
-        return cp
-
-    mine = w_ref.at[pl.ds(pl.multiple_of(core * half, half), half)]
-    w_up = send_w(0, mine, slot(yh, z), up)
-    w_down = send_w(1, mine, slot(yh, z), down)
-    w_cross = send_w(2, mine, slot(yh, z), cross)
-    sent = [w_up, w_down, w_cross]
-    shared = {}
-
-    def share(i, yh_, z_):
-        cp = send_w(i, slot(yh_, z_), slot(yh_, z_), sibling)
-        sent.append(cp)
-        return cp
-
-    def send_cot(k):
-        return remote(cot_ref, cot_all.at[x], c_send.at[k - 1], c_recv.at[k - 1], dev(x_=(x + k) % NX))
-
-    def send_normed(k):
-        return remote(nb.at[(x + k) % NX], nrecv.at[x], n_send.at[k - 1], n_recv.at[k - 1], dev(x_=(x + k) % NX))
-
-    for k in (1, 3, 2):
-        send_cot(k).start()
-
-    rate = jax.nn.softplus(dt_ref[...].astype(f32) + bias_ref[...])
+    rate = jax.nn.softplus(dt_ref[...].astype(f32).T + bias_ref[...])
     steps = rate * (-LOG2E * jnp.exp(al_ref[...]))
     row_pos = lax.broadcasted_iota(jnp.int32, (rows, rows), 0)
     col_pos = lax.broadcasted_iota(jnp.int32, (rows, rows), 1)
@@ -161,8 +126,10 @@
     for g in range(G):
         lg_ref[g] = log[:, g * HG : (g + 1) * HG]
         rg_ref[g] = rate[:, g * HG : (g + 1) * HG]
+        skip_ref[g] = skips_ref[:, g * HG : (g + 1) * HG]
         bg_ref[g] = b_ref[:, g * N : (g + 1) * N]
         cg_ref[g] = c_ref[:, g * N : (g + 1) * N]
+    x_copy.wait()
     for p in range(H // 2):
         lanes = slice(p * 128, (p + 1) * 128)
         xr = x_ref[:, lanes].astype(f32) * pair(rate, p, low)
@@ -177,6 +144,61 @@
         state = dot_tn(bg_ref[g], xw_ref[:, lanes])
         ext_ref[0:N, lanes] = state.astype(bf16)
 
+    own_w = pltpu.make_async_copy(w_ref, w_all.at[dp], local_sem.at[0])
+    own_w.start()
+    own_cot = pltpu.make_async_copy(cot_ref, cot_all.at[x], local_sem.at[1])
+    own_cot.start()
+    pl.semaphore_wait(barrier, NCTX - 1 + 5)
+
+    up_y = dev(yl_=1 - yl)
+    mine, theirs = yl, 1 - yl
+
+    def unit(yh_, z_, q, part=None):
+        start = core * half + q * quarter + (0 if part is None else part * (quarter // 2))
+        count = quarter if part is None else quarter // 2
+        return w_all.at[yh_ * NZ + z_, pl.ds(pl.multiple_of(start, quarter // 2), count)]
+
+    waits = {}
+    sent = []
+
+    def send_w(name, src, target, dst=None):
+        i = len(waits)
+        cp = remote(src, src if dst is None else dst, w_send.at[i], w_recv.at[i], target)
+        cp.start()
+        waits[name] = cp
+        sent.append(cp)
+
+    def arrived(*names):
+        for name in names:
+            waits[name].wait_recv()
+
+    def own_unit(q):
+        return w_ref.at[pl.ds(pl.multiple_of(core * half + q * quarter, quarter), quarter)]
+
+    def share(name, yh_, z_, q):
+        send_w(name, unit(yh_, z_, q), sibling)
+
+    def send_cot(k, part):
+        here = pl.ds(part * (rows // 2), rows // 2)
+        i = k - 1 + part
+        return remote(cot_ref.at[here], cot_all.at[x, here], c_send.at[i], c_recv.at[i], dev(x_=(x + k) % NX))
+
+    def hand_cot(part, side):
+        k = 1 + 2 * side
+        here = pl.ds(part * (rows // 2) + side * (rows // 4), rows // 4)
+        there = cot_all.at[(x + NX - k) % NX, here]
+        i = 4 + 2 * part + side
+        return remote(there, there, c_send.at[i], c_recv.at[i], dev(x_=(x + k) % NX))
+
+    def pass_cot(part):
+        for k in (1, 3):
+            send_cot(k, part).wait_recv()
+        for side in range(2):
+            hand_cot(part, side).start()
+
+    def send_normed(k):
+        return remote(nb.at[(x + k) % NX], nrecv.at[x], n_send.at[k - 1], n_recv.at[k - 1], dev(x_=(x + k) % NX))
+
     def lanes_of(j):
         return pl.ds(pl.multiple_of(j * SHARE, SHARE), SHARE)
 
@@ -215,6 +237,12 @@
     rev_out = lambda k: spread(gext_ref, gmine_ref, ga_send, ga_recv, k)
     rev_back = lambda k: back(link_ref, reach_ref, go_send, go_recv, k)
     start_all(fwd_out)
+    send_w("a1", own_unit(mine), up, unit(yh, z, mine))
+    send_w("a2", own_unit(mine), down, unit(yh, z, mine))
+    send_w("b1", own_unit(theirs), cross, unit(yh, z, theirs))
+    send_w("b2", own_unit(mine), cross, unit(yh, z, mine))
+    for k in (1, 3):
+        send_cot(k, 0).start()
     mine_ref[ctx] = ext_ref[:, lanes_of(ctx)]
 
     def within(g, _):
@@ -237,20 +265,26 @@
     link(False, mine_ref, link_ref, sin_ref)
     start_all(fwd_back)
 
-    w_up.wait_recv()
-    sent.append(send_w(3, slot(yh, z_down, 0, quarter), slot(yh, z_down, 0, quarter), up))
-    w_down.wait_recv()
-    sent.append(send_w(4, slot(yh, z_up, quarter, quarter), slot(yh, z_up, quarter, quarter), down))
-    w_cross.wait_recv()
-    sent.append(send_w(5, slot(1 - yh, z), slot(1 - yh, z), up))
-    sent.append(send_w(6, slot(1 - yh, z), slot(1 - yh, z), down))
-    w_far1, w_far2, w_cup, w_cdown = sent[3:7]
-    shared[0] = share(8, yh, z_down)
-    shared[1] = share(9, yh, z_up)
-    shared[2] = share(10, 1 - yh, z)
+    arrived("a1", "a2")
+    for name, z_ in (("n1", z_down), ("n2", z_up)):
+        send_w(name, unit(yh, z_, mine), up_y)
+    send_w("f1", unit(yh, z_down, mine, 0), up)
+    send_w("f2", unit(yh, z_up, mine, 1), down)
+    arrived("b1")
+    send_w("c1", unit(1 - yh, z, mine), up)
+    send_w("c2", unit(1 - yh, z, mine), down)
+    for name, z_ in (("m1", z_down), ("m2", z_up)):
+        send_w(name, unit(yh, z_, mine), cross)
+    share("s1", yh, z_down, mine)
+    share("s2", yh, z_up, mine)
+    share("s3", 1 - yh, z, mine)
+    pass_cot(0)
+    for k in (1, 3):
+        send_cot(k, 1).start()
 
     wait_recv_all(fwd_back)
 
+    z_copy.wait()
     acc_ref[...] = jnp.zeros_like(acc_ref)
 
     def gate(g, _):
@@ -302,30 +336,50 @@
         lax.fori_loop(0, 4, tile, 0)
 
     project(yh, z)
-    shared[0].wait_recv()
+    pass_cot(1)
+
+    arrived("f1", "f2")
+    share("s4", yh, z_far, mine)
+    arrived("b2")
+    share("s5", 1 - yh, z, theirs)
+    arrived("c1", "c2")
+    send_w("g1", unit(1 - yh, z_down, mine, 0), up)
+    send_w("g2", unit(1 - yh, z_up, mine, 1), down)
+    share("s6", 1 - yh, z_down, mine)
+    share("s7", 1 - yh, z_up, mine)
+    arrived("n1", "n2")
+    send_w("f3", unit(yh, z_down, theirs, 0), up)
+    send_w("f4", unit(yh, z_up, theirs, 1), down)
+    share("s8", yh, z_down, theirs)
+    share("s9", yh, z_up, theirs)
+    arrived("g1", "g2")
+    send_w("n4", unit(1 - yh, z_far, mine), up_y)
+    share("s10", 1 - yh, z_far, mine)
+    arrived("s3", "s5")
+    project(1 - yh, z)
+    arrived("s1", "s8")
     project(yh, z_down)
-    shared[1].wait_recv()
+    arrived("s2", "s9")
     project(yh, z_up)
-    shared[2].wait_recv()
-    project(1 - yh, z)
-    w_far1.wait_recv()
-    w_far2.wait_recv()
-    w_last = send_w(7, slot(yh, z_far), slot(yh, z_far), cross)
-    sent.append(w_last)
-    shared[3] = share(11, yh, z_far)
-    w_cup.wait_recv()
-    shared[4] = share(12, 1 - yh, z_down)
-    w_cdown.wait_recv()
-    shared[5] = share(13, 1 - yh, z_up)
-    shared[3].wait_recv()
+
+    arrived("m1", "m2")
+    share("s11", 1 - yh, z_down, theirs)
+    share("s12", 1 - yh, z_up, theirs)
+    arrived("f3", "f4")
+    share("s13", yh, z_far, theirs)
+    arrived("s6", "s11")
+    project(1 - yh, z_down)
+    arrived("s7", "s12")
+    project(1 - yh, z_up)
+    arrived("s4", "s13")
     project(yh, z_far)
-    shared[4].wait_recv()
-    project(1 - yh, z_down)
-    shared[5].wait_recv()
-    project(1 - yh, z_up)
-
+    arrived("n4")
+    share("s14", 1 - yh, z_far, theirs)
+
+    for part in range(2):
+        for side in range(2):
+            hand_cot(part, side).wait_recv()
     for k in (1, 3, 2):
-        send_cot(k).wait_recv()
         send_normed(k).wait_recv()
 
     def block_of(k):
@@ -348,39 +402,69 @@
 
         other_ref[i] = product(1 - core)
         send_half(k).start()
-        own_ref[i] = product(core)
+        own_ref[i // NZ, i % NZ] = product(core)
         return 0
 
     lax.fori_loop(0, NDP, weigh, 0)
-
-    def send_piece(k, j):
-        i = block_of(k)
-        other = (yl + j) % 2
-        return remote(own_ref.at[i, pl.ds(pl.multiple_of(other * 64, 64), 64)], rs_ref.at[dp * 2 + yl],
-                      r_send.at[2 * k + j], r_recv.at[2 * k + j], dev(yh_=i // NZ, z_=i % NZ, yl_=other))
 
     def combine(k, _):
         i = block_of(k)
         send_half(k).wait_recv()
-        own_ref[i] = (own_ref[i].astype(f32) + sib_ref[i].astype(f32)).astype(bf16)
-        return 0
-
-    def send_both(k, _):
-        combine(k, 0)
-        send_piece(k, 0).start()
-        send_piece(k, 1).start()
-        return 0
-
-    combine(0, 0)
-    send_piece(0, 1).start()
-    lax.fori_loop(1, NDP, send_both, 0)
-    rs_ref[dp * 2 + yl] = own_ref[dp, pl.ds(pl.multiple_of(yl * 64, 64), 64)]
-
-    w_last.wait_recv()
-    shared[6] = share(14, 1 - yh, z_far)
-    shared[6].wait_recv()
+        own_ref[i // NZ, i % NZ] = (own_ref[i // NZ, i % NZ].astype(f32) + sib_ref[i].astype(f32)).astype(bf16)
+        return 0
+
+    lax.fori_loop(0, NDP, combine, 0)
+
+    first, second = pl.ds(0, half_width // 2), pl.ds(half_width // 2, half_width // 2)
+    y = 2 * yh + yl
+
+    def rows_of(yl_):
+        return pl.ds(pl.multiple_of(yl_ * 64, 64), 64)
+
+    def reduce_copy(i, src, dst, target):
+        return remote(src, dst, r_send.at[i], r_recv.at[i], target)
+
+    def along_y(k):
+        there = (y + k) % 4
+        return there // 2, there % 2
+
+    def first_step():
+        copies = []
+        for k in (1, 3, 2):
+            yh_, yl_ = along_y(k)
+            copies.append(reduce_copy(k - 1, own_ref.at[yh_, :, rows_of(yl_), first], ra1_ref.at[y],
+                                      dev(yh_=yh_, yl_=yl_)))
+            z_ = (z + k) % NZ
+            copies.append(reduce_copy(k + 2, own_ref.at[:, z_, :, second], rb1_ref.at[z], dev(z_=z_)))
+        return copies
+
+    def second_step():
+        copies = []
+        for k in (1, 3, 2):
+            yh_, yl_ = along_y(k)
+            z_ = (z + k) % NZ
+            copies.append(reduce_copy(k + 5, ra1_ref.at[y, z_], ra2_ref.at[z], dev(z_=z_)))
+            copies.append(reduce_copy(k + 8, rb1_ref.at[z, yh_, rows_of(yl_)], rb2_ref.at[y],
+                                      dev(yh_=yh_, yl_=yl_)))
+        return copies
+
+    def total_of(ref):
+        total = ref[0].astype(f32)
+        for q in range(1, 4):
+            total = total + ref[q].astype(f32)
+        return total.astype(bf16)
+
+    step1 = first_step()
+    for cp in step1:
+        cp.start()
+    ra1_ref[y] = own_ref[yh, :, rows_of(yl), first]
+    rb1_ref[z] = own_ref[:, z, :, second]
+
+    arrived("s10", "s14")
     project(1 - yh, z_far)
     out_ref[...] = lay_ref[...].astype(bf16)
+    layer_copy = pltpu.make_async_copy(out_ref, layer_ref, local_sem.at[6])
+    layer_copy.start()
 
     acc_ref[...] = jnp.zeros_like(acc_ref)
 
@@ -417,8 +501,14 @@
         return 0
 
     lax.fori_loop(0, G, gate_back, 0)
+    dz_copy = pltpu.make_async_copy(dz_ref, dz_out, local_sem.at[7])
+    dz_copy.start()
     start_all(rev_out)
     gmine_ref[ctx] = gext_ref[:, lanes_of(ctx)]
+
+    e_pos = lax.broadcasted_iota(jnp.int32, (EG, HG), 0)
+    h_pos = lax.broadcasted_iota(jnp.int32, (EG, HG), 1)
+    heads = ((e_pos // P_SIZE) == h_pos).astype(bf16)
 
     def within_back(g, _):
         base = pl.multiple_of(g * EG, EG)
@@ -437,60 +527,73 @@
                 decays.append(decay)
                 parts.append((cbt * decay).astype(bf16))
             both = dot(jnp.concatenate(parts, axis=0), dy)
-            wide_ref[:, lanes] = jnp.where(low, both[:rows], both[rows:])
+            dxr = jnp.where(low, both[:rows], both[rows:])
+            wide_ref[:, lanes] = dxr
+            q1 = dy.astype(f32) * y_ref[:, lanes] - xr.astype(f32) * dxr
+            hi = q1.astype(bf16)
+            dn_ref[:, slice(p * 128, (p + 1) * 128)] = hi
+            dn_ref[:, slice(EG + p * 128, EG + (p + 1) * 128)] = (q1 - hi.astype(f32)).astype(bf16)
+            dn_ref[:, slice(2 * EG + p * 128, 2 * EG + (p + 1) * 128)] = (
+                x_ref[:, lanes].astype(f32) * dxr).astype(bf16)
             zero = jnp.zeros_like(xr)
             halves = jnp.concatenate([jnp.where(low, xr, zero), jnp.where(low, zero, xr)], axis=0)
             dm = dot_nt(halves, dy)
             add = dm[:rows] * decays[0] + dm[rows:] * decays[1]
             if p == 0:
-                dcb_ref[g] = add
+                dcb_ref[...] = add
             else:
-                dcb_ref[g] += add
+                dcb_ref[...] += add
+        wide = pl.ds(base, EG)
+        dcb = dcb_ref[...].astype(bf16)
+        dbg_ref[g] = dot(dcb, cg_ref[g])
+        qs_ref[g] = dot(dn_ref[:, 0:EG], heads) + dot(dn_ref[:, EG : 2 * EG], heads)
+        qs_ref[G + g] = dot(dn_ref[:, 2 * EG : 3 * EG], heads)
+        dcg_ref[g] = (dot_tn(dcb, bg_ref[g]) + dot_nt(dyel_ref[:, wide], sin_ref[:, wide])).astype(bf16)
         return 0
 
     lax.fori_loop(0, G // 2, within_back, 0)
+    for cp in step1:
+        cp.wait_recv()
+    ra1_ref[y] = total_of(ra1_ref)
+    rb1_ref[z] = total_of(rb1_ref)
+    step2 = second_step()
+    for cp in step2:
+        cp.start()
+    ra2_ref[z] = ra1_ref[y, z]
+    rb2_ref[y] = rb1_ref[z, yh, rows_of(yl)]
     wait_recv_all(rev_out)
     wait_send_all(fwd_back)
     link(True, gmine_ref, link_ref, reach_ref)
     start_all(rev_back)
     lax.fori_loop(G // 2, G, within_back, 0)
 
-    for k in range(NDP):
-        for j in range(2):
-            if k + j > 0:
-                send_piece(k, j).wait_recv()
-
-    total = rs_ref[0].astype(f32)
-    for q in range(1, 2 * NDP):
-        total = total + rs_ref[q].astype(f32)
-    piece_ref[...] = total.astype(bf16)
+    for cp in step2:
+        cp.wait_recv()
+    piece_ref[:, first] = total_of(ra2_ref)
+    piece_ref[:, second] = total_of(rb2_ref)
 
     def ring(k):
         return (x + k // 2) % NX, (yl + k) % 2
 
-    def ring_from(k):
-        return (x + NX - k // 2) % NX * 4 + (yl + k) % 2 * 2 + core
+    def place(x_, yl_):
+        rows_here = pl.ds(pl.multiple_of(x_ * 128 + yl_ * 64, 64), 64)
+        return gw_ref.at[rows_here, pl.ds(pl.multiple_of(core * half_width, half_width), half_width)]
 
     def send_sum(k):
         x_, yl_ = ring(k)
-        return remote(piece_ref, gw_ref.at[ctx], p_send.at[k], p_recv.at[k], dev(x_=x_, yl_=yl_))
+        return remote(piece_ref, place(x, yl), p_send.at[k], p_recv.at[k], dev(x_=x_, yl_=yl_))
 
     def hand_on(k):
-        src = gw_ref.at[ring_from(k)]
+        src = place((x + NX - k // 2) % NX, (yl + k) % 2)
         return remote(src, src, f_send.at[k], f_recv.at[k], sibling)
 
     for k in range(1, 2 * NX):
         send_sum(k).start()
-    to_sibling = remote(piece_ref, gw_ref.at[ctx], p_send.at[0], p_recv.at[0], sibling)
+    to_sibling = remote(piece_ref, place(x, yl), p_send.at[0], p_recv.at[0], sibling)
     to_sibling.start()
-    own_piece = pltpu.make_async_copy(piece_ref, gw_ref.at[ctx], local_sem.at[2])
+    own_piece = pltpu.make_async_copy(piece_ref, place(x, yl), local_sem.at[2])
     own_piece.start()
-
     wait_recv_all(rev_back)
-
-    e_pos = lax.broadcasted_iota(jnp.int32, (EG, HG), 0)
-    h_pos = lax.broadcasted_iota(jnp.int32, (EG, HG), 1)
-    heads = ((e_pos // P_SIZE) == h_pos).astype(bf16)
 
     def finish(g, _):
         base = pl.multiple_of(g * EG, EG)
@@ -498,45 +601,42 @@
         log = lg_ref[g]
         rate = rg_ref[g]
         b_blk = bg_ref[g]
-        c_blk = cg_ref[g]
         last = log[rows - 1 : rows, :]
         to_end = jnp.exp2(last - log)
         for p in range(HG // 2):
             here = slice(p * 128, (p + 1) * 128)
             lanes = pl.ds(pl.multiple_of(base + p * 128, 128), 128)
             dyf = dy_ref[:, lanes].astype(f32)
-            dxr = wide_ref[:, lanes] + pair(to_end, p, low) * dot(b_blk, reach_ref[:, lanes])
+            late = pair(to_end, p, low) * dot(b_blk, reach_ref[:, lanes])
+            dxr = wide_ref[:, lanes] + late
             dy_ref[:, lanes] = (dxr * pair(rate, p, low) + pair(skip_ref[g], p, low1) * dyf).astype(bf16)
-            q1 = dyf * y_ref[:, lanes] - xr_ref[:, lanes].astype(f32) * dxr
-            hi = q1.astype(bf16)
+            q2 = x_ref[:, lanes].astype(f32) * late
+            hi = q2.astype(bf16)
             dn_ref[:, here] = hi
-            dn_ref[:, slice(EG + p * 128, EG + (p + 1) * 128)] = (q1 - hi.astype(f32)).astype(bf16)
-            dn_ref[:, slice(2 * EG + p * 128, 2 * EG + (p + 1) * 128)] = (x_ref[:, lanes].astype(f32) * dxr).astype(bf16)
+            dn_ref[:, slice(EG + p * 128, EG + (p + 1) * 128)] = (q2 - hi.astype(f32)).astype(bf16)
         reach = reach_ref[:, wide]
-        dcb = dcb_ref[g].astype(bf16)
-        dbg_ref[g] = (dot(dcb, c_blk) + dot_nt(xw_ref[:, wide], reach)).astype(bf16)
-        dcg_ref[g] = (dot_tn(dcb, b_blk) + dot_nt(dyel_ref[:, wide], sin_ref[:, wide])).astype(bf16)
+        dbg_ref[g] += dot_nt(xw_ref[:, wide], reach)
         sums = []
         for v in (sin_ref[:, wide].astype(f32), ext_ref[0:N, wide].astype(f32)):
             v = jnp.sum(v * reach.astype(f32), axis=0, keepdims=True)
             a, b, _ = split3(jnp.broadcast_to(v, (16, EG)))
             sums.append((dot(a, heads) + dot(b, heads))[0:1])
         at_end = jnp.exp2(last) * sums[0] + sums[1]
-        q1 = dot(dn_ref[:, 0:EG], heads) + dot(dn_ref[:, EG : 2 * EG], heads)
-        qs_ref[g] = mask_dot(anticausal.astype(bf16), q1) + at_end
-        qs_ref[G + g] = dot(dn_ref[:, 2 * EG : 3 * EG], heads)
+        q2 = dot(dn_ref[:, 0:EG], heads) + dot(dn_ref[:, EG : 2 * EG], heads)
+        qs_ref[g] = mask_dot(anticausal.astype(bf16), qs_ref[g] - rate * q2) + at_end
+        qs_ref[G + g] += q2
         return 0
 
     lax.fori_loop(0, G, finish, 0)
     dx_out = pltpu.make_async_copy(dy_ref, dx_ref, local_sem.at[3])
     dx_out.start()
     a_neg = -jnp.exp(al_ref[...])
-    slope = jax.nn.sigmoid(dt_ref[...].astype(f32) + bias_ref[...])
+    slope = jax.nn.sigmoid(dt_ref[...].astype(f32).T + bias_ref[...])
     for g in range(G):
         here = slice(g * HG, (g + 1) * HG)
         d_rate = a_neg[:, here] * qs_ref[g] + qs_ref[G + g]
-        ddt_ref[:, here] = (d_rate * slope[:, here]).astype(bf16)
-        db_ref[:, g * N : (g + 1) * N] = dbg_ref[g]
+        ddt_ref[here, :] = (d_rate * slope[:, here]).T.astype(bf16)
+        db_ref[:, g * N : (g + 1) * N] = dbg_ref[g].astype(bf16)
         dc_ref[:, g * N : (g + 1) * N] = dcg_ref[g]
 
     for k in range(1, 2 * NX):
@@ -544,6 +644,8 @@
         hand_on(k).start()
 
     dx_out.wait()
+    layer_copy.wait()
+    dz_copy.wait()
     own_piece.wait()
     to_sibling.wait()
     for k in range(1, 2 * NX):
@@ -551,16 +653,48 @@
         hand_on(k).wait()
     for cp in sent:
         cp.wait_send()
+    for part in range(2):
+        for k in (1, 3):
+            send_cot(k, part).wait_send()
+        for side in range(2):
+            hand_cot(part, side).wait_send()
     for k in (1, 3, 2):
-        send_cot(k).wait_send()
         send_normed(k).wait_send()
     for make in (fwd_out, rev_out, rev_back):
         wait_send_all(make)
     for k in range(NDP):
         send_half(k).wait_send()
-        for j in range(2):
-            if k + j > 0:
-                send_piece(k, j).wait_send()
+    for cp in step1 + step2:
+        cp.wait_send()
+
+
+def result_kernel(*refs):
+    ins, outs = refs[:7], refs[7:14]
+    held = refs[14:20]
+    narrow, wide, sems, in_sems, out_sems = refs[20:]
+    rows = narrow.shape[0] // 4
+    loads = [pltpu.make_async_copy(ins[6].at[pl.ds(i * rows, rows)], narrow.at[pl.ds(i * rows, rows)], in_sems.at[i])
+             for i in range(4)]
+    for cp in loads:
+        cp.start()
+    arrays = [pltpu.make_async_copy(ins[i], held[i], sems.at[i]) for i in range(6)]
+    for cp in arrays:
+        cp.start()
+    copies = []
+    for i in range(4):
+        here = pl.ds(i * rows, rows)
+        loads[i].wait()
+        wide[here] = narrow[here].astype(f32)
+        cp = pltpu.make_async_copy(wide.at[here], outs[6].at[here], out_sems.at[i])
+        cp.start()
+        copies.append(cp)
+    for i in range(6):
+        arrays[i].wait()
+        cp = pltpu.make_async_copy(held[i], outs[i], sems.at[6 + i])
+        cp.start()
+        copies.append(cp)
+    for cp in copies:
+        cp.wait()
 
 
 def shards(xs, z_gate, b_proj, c_proj, dt_raw, a_log, dt_bias, d_skip, norm_gain, w_out, cotangent):
@@ -568,8 +702,8 @@
     width = cotangent.shape[2]
     shard = w_out.shape[0]
     wide = ((rows, E), bf16)
-    outs = [((rows, width), bf16), wide, wide, ((rows, G * N), bf16), ((rows, G * N), bf16), ((rows, H), bf16),
-            ((NCTX, shard // 8, width // 2), bf16)]
+    outs = [((rows, width), bf16), wide, wide, ((rows, G * N), bf16), ((rows, G * N), bf16), ((H, rows), bf16),
+            ((shard, width), bf16)]
     state = ((N, E), bf16)
     ext = ((EXT, E), bf16)
     share = ((NCTX, EXT, SHARE), bf16)
@@ -579,29 +713,40 @@
     quad = ((NX, rows, E // NX), bf16)
     block = ((NDP, 128, width // 2), bf16)
     scratch = [
+        wide, wide, ((rows, width), bf16), wide,
         ((NDP, shard, width), bf16), ((NX, rows, width), bf16), quad, quad, wide, wide, ((rows, E), f32),
         ((rows, E), f32), wide, wide, wide,
-        ((rows, width), f32), ((G, rows, rows), f32),
-        ((2 * G, rows, HG), f32), group_cols, group_cols,
-        per_group, per_group, ((H, rows), f32), group_cols, group_cols, ((rows, 128), f32),
+        ((rows, width), f32), ((rows, rows), f32),
+        ((2 * G, rows, HG), f32), ((G, rows, N), f32), group_cols,
+        per_group, per_group, ((H, rows), f32), group_cols, group_cols, ((rows, 128), f32), ((G, 1, HG), f32),
         ext, share, linked, state, ext, share, state,
-        block, block, block, ((2 * NDP, 64, width // 2), bf16), ((64, width // 2), bf16),
+        ((2, NZ, 128, width // 2), bf16), block, block, ((4, NZ, 64, width // 4), bf16), ((NZ, 2, 128, width // 4), bf16),
+        ((NZ, 64, width // 4), bf16), ((4, 64, width // 4), bf16), ((64, width // 2), bf16),
     ]
-    sems = [4, 15, 15, 3, 3, 3, 3] + [NCTX - 1] * 8 + [NDP, NDP, 2 * NDP, 2 * NDP] + [2 * NX] * 4
+    sems = [8, 32, 32, 8, 8, 3, 3] + [NCTX - 1] * 8 + [NDP, NDP, 12, 12] + [2 * NX] * 4
     vmem = pl.BlockSpec(memory_space=pltpu.VMEM)
     hbm = pl.BlockSpec(memory_space=pl.ANY)
     layer_out, dx, dz, db, dc, ddt, gw = pl.pallas_call(
         layer_kernel,
         out_shape=[jax.ShapeDtypeStruct(s, d) for s, d in outs],
-        in_specs=[vmem] * 9 + [hbm, hbm],
-        out_specs=[vmem, hbm] + [vmem] * 4 + [hbm],
+        in_specs=[hbm] * 2 + [vmem] * 7 + [hbm] * 2,
+        out_specs=[hbm] * 3 + [vmem] * 3 + [hbm],
         scratch_shapes=[pltpu.VMEM(s, d) for s, d in scratch] + [pltpu.SemaphoreType.DMA((n,)) for n in sems],
         compiler_params=pltpu.CompilerParams(
             collective_id=0, has_side_effects=True, vmem_limit_bytes=VMEM_LIMIT),
-    )(xs[0], z_gate[0], b_proj[0], c_proj[0], dt_raw[0], a_log[None], dt_bias[None],
-      d_skip.reshape(G, 1, HG), norm_gain[None], w_out, cotangent[0])
-    gw = gw.reshape(NX, 2, 2, 64, width // 2).transpose(0, 1, 3, 2, 4).reshape(shard, width).astype(f32)
-    return layer_out[None], dx[None], dz[None], db[None], dc[None], ddt[None], gw
+    )(xs[0], z_gate[0], b_proj[0], c_proj[0], dt_raw[0].T, a_log[None], dt_bias[None],
+      d_skip[None], norm_gain[None], w_out, cotangent[0])
+    layer_out, dx, dz, db, dc, ddt, gw = pl.pallas_call(
+        result_kernel,
+        out_shape=[jax.ShapeDtypeStruct(s, d) for s, d in outs[:6]] + [jax.ShapeDtypeStruct((shard, width), f32)],
+        in_specs=[hbm] * 7,
+        out_specs=[hbm] * 7,
+        scratch_shapes=[pltpu.VMEM(s, d) for s, d in outs[:6]]
+        + [pltpu.VMEM((shard, width), bf16), pltpu.VMEM((shard, width), f32), pltpu.SemaphoreType.DMA((12,)), pltpu.SemaphoreType.DMA((4,)),
+           pltpu.SemaphoreType.DMA((4,))],
+        compiler_params=pltpu.CompilerParams(vmem_limit_bytes=VMEM_LIMIT),
+    )(layer_out, dx, dz, db, dc, ddt, gw)
+    return layer_out[None], dx[None], dz[None], db[None], dc[None], ddt.T[None], gw
 
 
 def solution(mesh):

time: 188 us -> 137 us (0.73)
  Pallas kernels: 167 us -> 133 us
  local copies, waits for them, and re-layouts: 16.8 us -> 0 us
  other arithmetic: 2.05 us -> 0 us
    pallas_call x1, Pallas kernels: 167 us -> 128 us  [shards(): pl.pallas_call(layer_kernel, out_shape=[jax.ShapeDtypeStruct(s, d) for s,...]
    unnamed x18 -> x0, local copies, waits for them, and re-layouts: 12.2 us -> none
    pallas_call x0 -> x1, Pallas kernels: none -> 5.52 us  [shards(): pl.pallas_call(result_kernel, out_shape=[jax.ShapeDtypeStruct(s, d) for s...]
    convert_element_type x1 -> x0, local copies, waits for them, and re-layouts: 3.24 us -> none  [shards(): gw.reshape(NX, 2, 2, 64, width // 2).transpose(0, 1, 3, 2, 4)]
    convert_element_type x1 -> x0, other arithmetic: 2.05 us -> none  [shards(): gw.reshape(NX, 2, 2, 64, width // 2).transpose(0, 1, 3, 2, 4)]
where the time goes in v3:
time: 137 us; the launch traced here: 134 us
  Pallas kernels  133 us (97%)
    pallas_call x1, Pallas kernels, shards(): pl.pallas_call(layer_kernel, out_shape=[jax.ShapeDtypeStruct(s, d) for s,...  128 us
    pallas_call x1, Pallas kernels, shards(): pl.pallas_call(result_kernel, out_shape=[jax.ShapeDtypeStruct(s, d) for s...  5.52 us

profile of v3, /device:TPU:1, one launch (start us, length us, event | category | flops | bytes accessed | tf_op | source)
XLA Modules:
  0.0 134.1 jit_solution(675035519174020792)
XLA Ops:
  0.6 127.8 %shard_map.162 = (bf16[192,2048]{1,0:T(8,128)(2,1)}, bf16[192,4096]{1,0:T(8,128)(2,1)}, bf16[192,4096]{1,0:T(8,128)(2,1)}, bf16[192,256]{1,0:T(8,128)(2,1)}, bf1...) custom-call(bf16[192,4096]{1,0:T(8,128)(2,1)} %bitcast.20, bf16[192,4096]{1,0:T(8,128)(2,1)} %bitcast.21, ...), custom_call_target="tpu_custom_call" | custom-call | tf_op jit(solution)/shard_map/pallas_call | solution.py:729
  128.4 5.5 %shard_map.163 = (bf16[192,2048]{1,0:T(8,128)(2,1)}, bf16[192,4096]{1,0:T(8,128)(2,1)}, bf16[192,4096]{1,0:T(8,128)(2,1)}, bf16[192,256]{1,0:T(8,128)(2,1)}, bf1...) custom-call(bf16[192,2048]{1,0:T(8,128)(2,1)} %get-tuple-element.21.refs_0_, ...), custom_call_target="tpu_custom_call" | custom-call | tf_op jit(solution)/shard_map/pallas_call | solution.py:739

commit v4 on v3

--- a/solution.py
+++ b/solution.py
@@ -102,6 +102,9 @@
     z_copy = pltpu.make_async_copy(z_in, z_ref, local_sem.at[5])
     z_copy.start()
 
+    def tokens(x_, start=0, count=rows):
+        return pl.ds(pl.multiple_of(x_ * rows + start, 16), count)
+
     barrier = pltpu.get_barrier_semaphore()
 
     def greet_ctx(k, _):
@@ -129,6 +132,70 @@
         skip_ref[g] = skips_ref[:, g * HG : (g + 1) * HG]
         bg_ref[g] = b_ref[:, g * N : (g + 1) * N]
         cg_ref[g] = c_ref[:, g * N : (g + 1) * N]
+    own_w = pltpu.make_async_copy(w_ref, w_all.at[dp], local_sem.at[0])
+    own_w.start()
+    own_cot = pltpu.make_async_copy(cot_ref, cot_all.at[tokens(x)], local_sem.at[1])
+    own_cot.start()
+    pl.semaphore_wait(barrier, NCTX - 1 + 5)
+
+    up_y = dev(yl_=1 - yl)
+    mine, theirs = yl, 1 - yl
+
+    def unit(yh_, z_, q, part=None):
+        start = core * half + q * quarter + (0 if part is None else part * (quarter // 2))
+        count = quarter if part is None else quarter // 2
+        return w_all.at[yh_ * NZ + z_, pl.ds(pl.multiple_of(start, quarter // 2), count)]
+
+    waits = {}
+    sent = []
+
+    def send_w(name, src, target, dst=None):
+        i = len(waits)
+        cp = remote(src, src if dst is None else dst, w_send.at[i], w_recv.at[i], target)
+        cp.start()
+        waits[name] = cp
+        sent.append(cp)
+
+    def arrived(*names):
+        for name in names:
+            waits[name].wait_recv()
+
+    def own_unit(q, part=None):
+        start = core * half + q * quarter + (0 if part is None else part * (quarter // 2))
+        count = quarter if part is None else quarter // 2
+        return w_ref.at[pl.ds(pl.multiple_of(start, quarter // 2), count)]
+
+    def share(name, yh_, z_, q):
+        send_w(name, unit(yh_, z_, q), sibling)
+
+    def send_cot(k, part):
+        here = pl.ds(part * (rows // 2), rows // 2)
+        i = k - 1 + part
+        return remote(cot_ref.at[here], cot_all.at[tokens(x, part * (rows // 2), rows // 2)], c_send.at[i], c_recv.at[i], dev(x_=(x + k) % NX))
+
+    def hand_cot(part, side):
+        k = 1 + 2 * side
+        there = cot_all.at[tokens((x + NX - k) % NX, part * (rows // 2) + side * (rows // 4), rows // 4)]
+        i = 4 + 2 * part + side
+        return remote(there, there, c_send.at[i], c_recv.at[i], dev(x_=(x + k) % NX))
+
+    def pass_cot(part):
+        for k in (1, 3):
+            send_cot(k, part).wait_recv()
+        for side in range(2):
+            hand_cot(part, side).start()
+
+    def send_normed(k):
+        return remote(nb.at[(x + k) % NX], nrecv.at[tokens(x)], n_send.at[k - 1], n_recv.at[k - 1], dev(x_=(x + k) % NX))
+
+    send_w("a1", own_unit(mine), up, unit(yh, z, mine))
+    send_w("a2", own_unit(mine), down, unit(yh, z, mine))
+    send_w("b1", own_unit(theirs), cross, unit(yh, z, theirs))
+    send_w("e1", own_unit(theirs, 1), up, unit(yh, z, theirs, 1))
+    send_w("e2", own_unit(theirs, 1), down, unit(yh, z, theirs, 1))
+    send_w("b2", own_unit(mine), cross, unit(yh, z, mine))
+    for k in (1, 3):
+        send_cot(k, 0).start()
     x_copy.wait()
     for p in range(H // 2):
         lanes = slice(p * 128, (p + 1) * 128)
@@ -138,66 +205,10 @@
         hi, mid, lo = split3(pair(last, p, low1))
         tail = jnp.concatenate([hi, mid, lo, jnp.zeros((EXT - N - 3, 128), bf16)], axis=0)
         ext_ref[N:EXT, lanes] = tail
-        gext_ref[N:EXT, lanes] = tail
     for g in range(G):
         lanes = slice(g * EG, (g + 1) * EG)
         state = dot_tn(bg_ref[g], xw_ref[:, lanes])
         ext_ref[0:N, lanes] = state.astype(bf16)
-
-    own_w = pltpu.make_async_copy(w_ref, w_all.at[dp], local_sem.at[0])
-    own_w.start()
-    own_cot = pltpu.make_async_copy(cot_ref, cot_all.at[x], local_sem.at[1])
-    own_cot.start()
-    pl.semaphore_wait(barrier, NCTX - 1 + 5)
-
-    up_y = dev(yl_=1 - yl)
-    mine, theirs = yl, 1 - yl
-
-    def unit(yh_, z_, q, part=None):
-        start = core * half + q * quarter + (0 if part is None else part * (quarter // 2))
-        count = quarter if part is None else quarter // 2
-        return w_all.at[yh_ * NZ + z_, pl.ds(pl.multiple_of(start, quarter // 2), count)]
-
-    waits = {}
-    sent = []
-
-    def send_w(name, src, target, dst=None):
-        i = len(waits)
-        cp = remote(src, src if dst is None else dst, w_send.at[i], w_recv.at[i], target)
-        cp.start()
-        waits[name] = cp
-        sent.append(cp)
-
-    def arrived(*names):
-        for name in names:
-            waits[name].wait_recv()
-
-    def own_unit(q):
-        return w_ref.at[pl.ds(pl.multiple_of(core * half + q * quarter, quarter), quarter)]
-
-    def share(name, yh_, z_, q):
-        send_w(name, unit(yh_, z_, q), sibling)
-
-    def send_cot(k, part):
-        here = pl.ds(part * (rows // 2), rows // 2)
-        i = k - 1 + part
-        return remote(cot_ref.at[here], cot_all.at[x, here], c_send.at[i], c_recv.at[i], dev(x_=(x + k) % NX))
-
-    def hand_cot(part, side):
-        k = 1 + 2 * side
-        here = pl.ds(part * (rows // 2) + side * (rows // 4), rows // 4)
-        there = cot_all.at[(x + NX - k) % NX, here]
-        i = 4 + 2 * part + side
-        return remote(there, there, c_send.at[i], c_recv.at[i], dev(x_=(x + k) % NX))
-
-    def pass_cot(part):
-        for k in (1, 3):
-            send_cot(k, part).wait_recv()
-        for side in range(2):
-            hand_cot(part, side).start()
-
-    def send_normed(k):
-        return remote(nb.at[(x + k) % NX], nrecv.at[x], n_send.at[k - 1], n_recv.at[k - 1], dev(x_=(x + k) % NX))
 
     def lanes_of(j):
         return pl.ds(pl.multiple_of(j * SHARE, SHARE), SHARE)
@@ -227,9 +238,9 @@
         for step in range(NCTX):
             j = NCTX - 1 - step if reverse else step
             linked[j] = acc.astype(bf16)
-            part = gathered[j].astype(f32)
-            total = part[N : N + 1] + part[N + 1 : N + 2] + part[N + 2 : N + 3]
-            acc = jnp.exp2(total) * acc + part[0:N]
+            tail = mine_ref[j, N:EXT, :].astype(f32)
+            total = tail[0:1] + tail[1:2] + tail[2:3]
+            acc = jnp.exp2(total) * acc + gathered[j, 0:N, :].astype(f32)
         into[:, lanes_of(ctx)] = linked[ctx]
 
     fwd_out = lambda k: spread(ext_ref, mine_ref, a_send, a_recv, k)
@@ -237,12 +248,6 @@
     rev_out = lambda k: spread(gext_ref, gmine_ref, ga_send, ga_recv, k)
     rev_back = lambda k: back(link_ref, reach_ref, go_send, go_recv, k)
     start_all(fwd_out)
-    send_w("a1", own_unit(mine), up, unit(yh, z, mine))
-    send_w("a2", own_unit(mine), down, unit(yh, z, mine))
-    send_w("b1", own_unit(theirs), cross, unit(yh, z, theirs))
-    send_w("b2", own_unit(mine), cross, unit(yh, z, mine))
-    for k in (1, 3):
-        send_cot(k, 0).start()
     mine_ref[ctx] = ext_ref[:, lanes_of(ctx)]
 
     def within(g, _):
@@ -265,14 +270,12 @@
     link(False, mine_ref, link_ref, sin_ref)
     start_all(fwd_back)
 
-    arrived("a1", "a2")
-    for name, z_ in (("n1", z_down), ("n2", z_up)):
-        send_w(name, unit(yh, z_, mine), up_y)
-    send_w("f1", unit(yh, z_down, mine, 0), up)
-    send_w("f2", unit(yh, z_up, mine, 1), down)
     arrived("b1")
     send_w("c1", unit(1 - yh, z, mine), up)
     send_w("c2", unit(1 - yh, z, mine), down)
+    arrived("a1", "a2")
+    for name, z_ in (("n1", z_down), ("n2", z_up)):
+        send_w(name, unit(yh, z_, mine, 0), up_y)
     for name, z_ in (("m1", z_down), ("m2", z_up)):
         send_w(name, unit(yh, z_, mine), cross)
     share("s1", yh, z_down, mine)
@@ -317,15 +320,26 @@
     lax.fori_loop(0, NDP, norm, 0)
     for k in (1, 3, 2):
         send_normed(k).start()
-    nrecv[x] = nb[x]
+    nrecv[tokens(x)] = nb[x]
 
     own_w.wait()
     own_cot.wait()
     lay_ref[...] = jnp.zeros_like(lay_ref)
 
-    def project(yh_, z_):
+    acc_ref[...] = jnp.zeros_like(acc_ref)
+
+    def project_back(yh_, z_):
         k = yh_ * NZ + z_
-        dn_ref[:, pl.ds(pl.multiple_of(k * shard, shard), shard)] = dot_nt(cot_all[x], w_all[k]).astype(bf16)
+        acc = acc_ref[...]
+        for q in range(NX):
+            lanes = pl.ds(pl.multiple_of(k * shard + q * 128, 128), 128)
+            dn = dot_nt(cot_all[tokens(x)], w_all[k, q * 128 : (q + 1) * 128, :]).astype(bf16)
+            dn_ref[:, lanes] = dn
+            acc = acc + dn.astype(f32) * gain_ref[:, lanes] * wide_ref[:, lanes]
+        acc_ref[...] = acc
+
+    def project_out(yh_, z_):
+        k = yh_ * NZ + z_
         block = jnp.concatenate([nb[q, :, pl.ds(pl.multiple_of(k * 128, 128), 128)] for q in range(NX)], axis=1)
 
         def tile(n, _):
@@ -335,28 +349,34 @@
 
         lax.fori_loop(0, 4, tile, 0)
 
+    def project(yh_, z_):
+        project_back(yh_, z_)
+        project_out(yh_, z_)
+
     project(yh, z)
-    pass_cot(1)
-
-    arrived("f1", "f2")
-    share("s4", yh, z_far, mine)
-    arrived("b2")
-    share("s5", 1 - yh, z, theirs)
+
     arrived("c1", "c2")
     send_w("g1", unit(1 - yh, z_down, mine, 0), up)
     send_w("g2", unit(1 - yh, z_up, mine, 1), down)
+    send_w("f1", unit(yh, z_down, mine, 0), up)
+    send_w("f2", unit(yh, z_up, mine, 1), down)
+    arrived("e2")
+    send_w("f4", unit(yh, z_up, theirs, 1), down)
     share("s6", 1 - yh, z_down, mine)
     share("s7", 1 - yh, z_up, mine)
-    arrived("n1", "n2")
+    arrived("b2")
+    share("s5", 1 - yh, z, theirs)
+    pass_cot(1)
+    arrived("n1")
     send_w("f3", unit(yh, z_down, theirs, 0), up)
-    send_w("f4", unit(yh, z_up, theirs, 1), down)
+    arrived("n2", "e1")
     share("s8", yh, z_down, theirs)
     share("s9", yh, z_up, theirs)
+    arrived("s3", "s5")
+    project(1 - yh, z)
     arrived("g1", "g2")
     send_w("n4", unit(1 - yh, z_far, mine), up_y)
     share("s10", 1 - yh, z_far, mine)
-    arrived("s3", "s5")
-    project(1 - yh, z)
     arrived("s1", "s8")
     project(yh, z_down)
     arrived("s2", "s9")
@@ -365,10 +385,12 @@
     arrived("m1", "m2")
     share("s11", 1 - yh, z_down, theirs)
     share("s12", 1 - yh, z_up, theirs)
+    arrived("f1", "f2")
+    share("s4", yh, z_far, mine)
+    arrived("s6", "s11")
+    project(1 - yh, z_down)
     arrived("f3", "f4")
     share("s13", yh, z_far, theirs)
-    arrived("s6", "s11")
-    project(1 - yh, z_down)
     arrived("s7", "s12")
     project(1 - yh, z_up)
     arrived("s4", "s13")
@@ -382,41 +404,46 @@
     for k in (1, 3, 2):
         send_normed(k).wait_recv()
 
-    def block_of(k):
-        return (dp + k) % NDP
-
-    def send_half(k):
-        i = block_of(k)
-        return remote(other_ref.at[i], sib_ref.at[i], b_send.at[k], b_recv.at[k], sibling)
-
-    def weigh(k, _):
-        i = block_of(k)
-        lanes = pl.ds(pl.multiple_of(i * 128, 128), 128)
-
-        def product(side):
-            cols = pl.ds(pl.multiple_of(side * half_width, half_width), half_width)
-            total = dot_tn(nrecv[0, :, lanes], cot_all[0, :, cols])
-            for s in range(1, NX):
-                total = total + dot_tn(nrecv[s, :, lanes], cot_all[s, :, cols])
-            return total.astype(bf16)
-
-        other_ref[i] = product(1 - core)
-        send_half(k).start()
-        own_ref[i // NZ, i % NZ] = product(core)
-        return 0
-
-    lax.fori_loop(0, NDP, weigh, 0)
-
-    def combine(k, _):
-        i = block_of(k)
-        send_half(k).wait_recv()
-        own_ref[i // NZ, i % NZ] = (own_ref[i // NZ, i % NZ].astype(f32) + sib_ref[i].astype(f32)).astype(bf16)
-        return 0
-
-    lax.fori_loop(0, NDP, combine, 0)
-
-    first, second = pl.ds(0, half_width // 2), pl.ds(half_width // 2, half_width // 2)
+    def send_half(j):
+        return remote(other_ref.at[j], sib_ref.at[j], b_send.at[j], b_recv.at[j], sibling)
+
+    def product(j, side):
+        cols = pl.ds(pl.multiple_of(side * half_width, half_width), half_width)
+        return dot_tn(nrecv[:, pl.ds(pl.multiple_of(j * 256, 256), 256)], cot_all[:, cols]).astype(bf16)
+
+    def weigh_other(j, _):
+        other_ref[j] = product(j, 1 - core)
+        send_half(j).start()
+        return 0
+
+    def weigh_own(j, _):
+        part = product(j, core)
+        own_ref[j // 2, 2 * (j % 2)] = part[0:128]
+        own_ref[j // 2, 2 * (j % 2) + 1] = part[128:256]
+        return 0
+
+    def combine(j, _):
+        send_half(j).wait_recv()
+        for i in range(2):
+            here = (j // 2, 2 * (j % 2) + i)
+            got = sib_ref[j, i * 128 : (i + 1) * 128, :]
+            own_ref[here] = (own_ref[here].astype(f32) + got.astype(f32)).astype(bf16)
+        return 0
+
+    lax.fori_loop(0, NDP // 2, weigh_other, 0)
+    lax.fori_loop(0, NDP // 2, weigh_own, 0)
+    lax.fori_loop(0, NDP // 2, combine, 0)
+
     y = 2 * yh + yl
+    part_width = half_width // 2
+    y_span = part_width // 4
+    z_span = part_width - y_span
+
+    def y_first(part, start=0):
+        return pl.ds(part * start + part * (0 if start else y_span), y_span)
+
+    def z_first(part, start=0):
+        return pl.ds(part * start + (y_span if start else part * z_span), z_span)
 
     def rows_of(yl_):
         return pl.ds(pl.multiple_of(yl_ * 64, 64), 64)
@@ -428,56 +455,88 @@
         there = (y + k) % 4
         return there // 2, there % 2
 
-    def first_step():
+    def first_step(part):
         copies = []
         for k in (1, 3, 2):
             yh_, yl_ = along_y(k)
-            copies.append(reduce_copy(k - 1, own_ref.at[yh_, :, rows_of(yl_), first], ra1_ref.at[y],
-                                      dev(yh_=yh_, yl_=yl_)))
+            copies.append(reduce_copy(12 * part + k - 1, own_ref.at[yh_, :, rows_of(yl_), y_first(part, part_width)],
+                                      ra1_ref.at[y, :, :, y_first(part)], dev(yh_=yh_, yl_=yl_)))
             z_ = (z + k) % NZ
-            copies.append(reduce_copy(k + 2, own_ref.at[:, z_, :, second], rb1_ref.at[z], dev(z_=z_)))
+            copies.append(reduce_copy(12 * part + k + 2, own_ref.at[:, z_, :, z_first(part, part_width)],
+                                      rb1_ref.at[z, :, :, z_first(part)], dev(z_=z_)))
+        for cp in copies:
+            cp.start()
         return copies
 
-    def second_step():
+    def total_of(ref, here):
+        total = ref[(0, Ellipsis, here)].astype(f32)
+        for q in range(1, 4):
+            total = total + ref[(q, Ellipsis, here)].astype(f32)
+        return total.astype(bf16)
+
+    def second_step(part):
+        for cp in step1[part]:
+            cp.wait_recv()
+        ya, za = y_first(part), z_first(part)
+        ra1_ref[y, :, :, ya] = total_of(ra1_ref, ya)
+        rb1_ref[z, :, :, za] = total_of(rb1_ref, za)
         copies = []
         for k in (1, 3, 2):
             yh_, yl_ = along_y(k)
             z_ = (z + k) % NZ
-            copies.append(reduce_copy(k + 5, ra1_ref.at[y, z_], ra2_ref.at[z], dev(z_=z_)))
-            copies.append(reduce_copy(k + 8, rb1_ref.at[z, yh_, rows_of(yl_)], rb2_ref.at[y],
-                                      dev(yh_=yh_, yl_=yl_)))
+            copies.append(reduce_copy(12 * part + k + 5, ra1_ref.at[y, z_, :, ya], ra2_ref.at[z, :, ya],
+                                      dev(z_=z_)))
+            copies.append(reduce_copy(12 * part + k + 8, rb1_ref.at[z, yh_, rows_of(yl_), za],
+                                      rb2_ref.at[y, :, za], dev(yh_=yh_, yl_=yl_)))
+        for cp in copies:
+            cp.start()
+        ra2_ref[z, :, ya] = ra1_ref[y, z, :, ya]
+        rb2_ref[y, :, za] = rb1_ref[z, yh, rows_of(yl), za]
         return copies
 
-    def total_of(ref):
-        total = ref[0].astype(f32)
-        for q in range(1, 4):
-            total = total + ref[q].astype(f32)
-        return total.astype(bf16)
-
-    step1 = first_step()
-    for cp in step1:
-        cp.start()
-    ra1_ref[y] = own_ref[yh, :, rows_of(yl), first]
-    rb1_ref[z] = own_ref[:, z, :, second]
+    def place(x_, yl_, part):
+        rows_here = pl.ds(pl.multiple_of(x_ * 128 + yl_ * 64, 64), 64)
+        start = core * half_width + part * (half_width // 2)
+        return gw_ref.at[rows_here, pl.ds(pl.multiple_of(start, half_width // 2), half_width // 2)]
+
+    def own_cols(part):
+        return piece_ref.at[:, pl.ds(part * (half_width // 2), half_width // 2)]
+
+    def send_sum(k, part):
+        i = 8 * part + k
+        target = sibling if k == 0 else dev(x_=(x + k // 2) % NX, yl_=(yl + k) % 2)
+        return remote(own_cols(part), place(x, yl, part), p_send.at[i], p_recv.at[i], target)
+
+    def hand_on(k, part):
+        src = place((x + NX - k // 2) % NX, (yl + k) % 2, part)
+        i = 8 * part + k
+        return remote(src, src, f_send.at[i], f_recv.at[i], sibling)
+
+    def own_piece(part):
+        return pltpu.make_async_copy(own_cols(part), place(x, yl, part), local_sem.at[2 + 6 * part])
+
+    def spread_sum(part):
+        for cp in step2[part]:
+            cp.wait_recv()
+        piece_ref[:, y_first(part, part_width)] = total_of(ra2_ref, y_first(part))
+        piece_ref[:, z_first(part, part_width)] = total_of(rb2_ref, z_first(part))
+        for k in (2, 6, 4, 1, 3, 7, 5, 0):
+            send_sum(k, part).start()
+        own_piece(part).start()
+
+    def hand_all(part):
+        for k in (2, 6, 1, 3, 7, 4, 5):
+            send_sum(k, part).wait_recv()
+            hand_on(k, part).start()
+
+    step1 = [first_step(0), first_step(1)]
+    for part in range(2):
+        ra1_ref[y, :, :, y_first(part)] = own_ref[yh, :, rows_of(yl), y_first(part, part_width)]
+        rb1_ref[z, :, :, z_first(part)] = own_ref[:, z, :, z_first(part, part_width)]
 
     arrived("s10", "s14")
-    project(1 - yh, z_far)
-    out_ref[...] = lay_ref[...].astype(bf16)
-    layer_copy = pltpu.make_async_copy(out_ref, layer_ref, local_sem.at[6])
-    layer_copy.start()
-
-    acc_ref[...] = jnp.zeros_like(acc_ref)
-
-    def mean(g, _):
-        base = pl.multiple_of(g * EG, EG)
-        acc = acc_ref[...]
-        for p in range(HG // 2):
-            lanes = pl.ds(pl.multiple_of(base + p * 128, 128), 128)
-            acc = acc + dn_ref[:, lanes].astype(f32) * gain_ref[:, lanes] * wide_ref[:, lanes]
-        acc_ref[...] = acc
-        return 0
-
-    lax.fori_loop(0, G, mean, 0)
+    project_back(1 - yh, z_far)
+
     inner = jnp.sum(acc_ref[...], axis=1, keepdims=True) * (1.0 / E)
     scaled = r * r * inner
 
@@ -497,7 +556,7 @@
             dy_ref[:, lanes] = dy.astype(bf16)
             dyel_ref[:, lanes] = (dy * pair(grown, p, low)).astype(bf16)
         lanes = pl.ds(base, EG)
-        gext_ref[0:N, lanes] = dot_tn(cg_ref[g], dyel_ref[:, lanes]).astype(bf16)
+        gext_ref[:, lanes] = dot_tn(cg_ref[g], dyel_ref[:, lanes]).astype(bf16)
         return 0
 
     lax.fori_loop(0, G, gate_back, 0)
@@ -505,6 +564,10 @@
     dz_copy.start()
     start_all(rev_out)
     gmine_ref[ctx] = gext_ref[:, lanes_of(ctx)]
+    project_out(1 - yh, z_far)
+    out_ref[...] = lay_ref[...].astype(bf16)
+    layer_copy = pltpu.make_async_copy(out_ref, layer_ref, local_sem.at[6])
+    layer_copy.start()
 
     e_pos = lax.broadcasted_iota(jnp.int32, (EG, HG), 0)
     h_pos = lax.broadcasted_iota(jnp.int32, (EG, HG), 1)
@@ -552,47 +615,15 @@
         return 0
 
     lax.fori_loop(0, G // 2, within_back, 0)
-    for cp in step1:
-        cp.wait_recv()
-    ra1_ref[y] = total_of(ra1_ref)
-    rb1_ref[z] = total_of(rb1_ref)
-    step2 = second_step()
-    for cp in step2:
-        cp.start()
-    ra2_ref[z] = ra1_ref[y, z]
-    rb2_ref[y] = rb1_ref[z, yh, rows_of(yl)]
+    step2 = [second_step(0)]
+    lax.fori_loop(G // 2, G, within_back, 0)
     wait_recv_all(rev_out)
     wait_send_all(fwd_back)
     link(True, gmine_ref, link_ref, reach_ref)
     start_all(rev_back)
-    lax.fori_loop(G // 2, G, within_back, 0)
-
-    for cp in step2:
-        cp.wait_recv()
-    piece_ref[:, first] = total_of(ra2_ref)
-    piece_ref[:, second] = total_of(rb2_ref)
-
-    def ring(k):
-        return (x + k // 2) % NX, (yl + k) % 2
-
-    def place(x_, yl_):
-        rows_here = pl.ds(pl.multiple_of(x_ * 128 + yl_ * 64, 64), 64)
-        return gw_ref.at[rows_here, pl.ds(pl.multiple_of(core * half_width, half_width), half_width)]
-
-    def send_sum(k):
-        x_, yl_ = ring(k)
-        return remote(piece_ref, place(x, yl), p_send.at[k], p_recv.at[k], dev(x_=x_, yl_=yl_))
-
-    def hand_on(k):
-        src = place((x + NX - k // 2) % NX, (yl + k) % 2)
-        return remote(src, src, f_send.at[k], f_recv.at[k], sibling)
-
-    for k in range(1, 2 * NX):
-        send_sum(k).start()
-    to_sibling = remote(piece_ref, place(x, yl), p_send.at[0], p_recv.at[0], sibling)
-    to_sibling.start()
-    own_piece = pltpu.make_async_copy(piece_ref, place(x, yl), local_sem.at[2])
-    own_piece.start()
+
+    step2.append(second_step(1))
+    spread_sum(0)
     wait_recv_all(rev_back)
 
     def finish(g, _):
@@ -627,7 +658,10 @@
         qs_ref[G + g] += q2
         return 0
 
-    lax.fori_loop(0, G, finish, 0)
+    lax.fori_loop(0, G // 2, finish, 0)
+    spread_sum(1)
+    lax.fori_loop(G // 2, G, finish, 0)
+    hand_all(0)
     dx_out = pltpu.make_async_copy(dy_ref, dx_ref, local_sem.at[3])
     dx_out.start()
     a_neg = -jnp.exp(al_ref[...])
@@ -639,18 +673,17 @@
         db_ref[:, g * N : (g + 1) * N] = dbg_ref[g].astype(bf16)
         dc_ref[:, g * N : (g + 1) * N] = dcg_ref[g]
 
-    for k in range(1, 2 * NX):
-        send_sum(k).wait_recv()
-        hand_on(k).start()
+    hand_all(1)
 
     dx_out.wait()
     layer_copy.wait()
     dz_copy.wait()
-    own_piece.wait()
-    to_sibling.wait()
-    for k in range(1, 2 * NX):
-        send_sum(k).wait_send()
-        hand_on(k).wait()
+    for part in range(2):
+        own_piece(part).wait()
+        send_sum(0, part).wait()
+        for k in range(1, 2 * NX):
+            send_sum(k, part).wait_send()
+            hand_on(k, part).wait()
     for cp in sent:
         cp.wait_send()
     for part in range(2):
@@ -662,10 +695,11 @@
         send_normed(k).wait_send()
     for make in (fwd_out, rev_out, rev_back):
         wait_send_all(make)
-    for k in range(NDP):
+    for k in range(NDP // 2):
         send_half(k).wait_send()
-    for cp in step1 + step2:
-        cp.wait_send()
+    for copies in step1 + step2:
+        for cp in copies:
+            cp.wait_send()
 
 
 def result_kernel(*refs):
@@ -711,19 +745,19 @@
     per_group = ((G, rows, HG), f32)
     group_cols = ((G, rows, N), bf16)
     quad = ((NX, rows, E // NX), bf16)
-    block = ((NDP, 128, width // 2), bf16)
+    block = ((NDP // 2, 256, width // 2), bf16)
     scratch = [
         wide, wide, ((rows, width), bf16), wide,
-        ((NDP, shard, width), bf16), ((NX, rows, width), bf16), quad, quad, wide, wide, ((rows, E), f32),
+        ((NDP, shard, width), bf16), ((NX * rows, width), bf16), quad, ((NX * rows, E // NX), bf16), wide, wide, ((rows, E), f32),
         ((rows, E), f32), wide, wide, wide,
         ((rows, width), f32), ((rows, rows), f32),
         ((2 * G, rows, HG), f32), ((G, rows, N), f32), group_cols,
         per_group, per_group, ((H, rows), f32), group_cols, group_cols, ((rows, 128), f32), ((G, 1, HG), f32),
-        ext, share, linked, state, ext, share, state,
-        ((2, NZ, 128, width // 2), bf16), block, block, ((4, NZ, 64, width // 4), bf16), ((NZ, 2, 128, width // 4), bf16),
-        ((NZ, 64, width // 4), bf16), ((4, 64, width // 4), bf16), ((64, width // 2), bf16),
+        ext, share, linked, state, state, linked, state,
+        ((2, NZ, 128, width // 2), bf16), block, block, ((4, NZ, 64, width // 8), bf16), ((NZ, 2, 128, 3 * width // 8), bf16),
+        ((NZ, 64, width // 8), bf16), ((4, 64, 3 * width // 8), bf16), ((64, width // 2), bf16),
     ]
-    sems = [8, 32, 32, 8, 8, 3, 3] + [NCTX - 1] * 8 + [NDP, NDP, 12, 12] + [2 * NX] * 4
+    sems = [9, 36, 36, 8, 8, 3, 3] + [NCTX - 1] * 8 + [NDP // 2, NDP // 2, 24, 24] + [4 * NX] * 4
     vmem = pl.BlockSpec(memory_space=pltpu.VMEM)
     hbm = pl.BlockSpec(memory_space=pl.ANY)
     layer_out, dx, dz, db, dc, ddt, gw = pl.pallas_call(

time: 137 us -> 126 us (0.920); the launches traced: 134 us -> 125 us
  Pallas kernels: 133 us -> 125 us
    pallas_call x1, Pallas kernels: 128 us -> 119 us  [shards(): pl.pallas_call(layer_kernel, out_shape=[jax.ShapeDtypeStruct(s, d) for s,...]
where the time goes in v4:
time: 126 us; the launch traced here: 125 us
  Pallas kernels  125 us (99%)
    pallas_call x1, Pallas kernels, shards(): pl.pallas_call(layer_kernel, out_shape=[jax.ShapeDtypeStruct(s, d) for s,...  119 us
    pallas_call x1, Pallas kernels, shards(): pl.pallas_call(result_kernel, out_shape=[jax.ShapeDtypeStruct(s, d) for s...  5.52 us

profile of v4, /device:TPU:1, one launch (start us, length us, event | category | flops | bytes accessed | tf_op | source)
XLA Modules:
  0.0 125.5 jit_solution(388349288044305364)
XLA Ops:
  0.6 119.2 %shard_map.162 = (bf16[192,2048]{1,0:T(8,128)(2,1)}, bf16[192,4096]{1,0:T(8,128)(2,1)}, bf16[192,4096]{1,0:T(8,128)(2,1)}, bf16[192,256]{1,0:T(8,128)(2,1)}, bf1...) custom-call(bf16[192,4096]{1,0:T(8,128)(2,1)} %bitcast.20, bf16[192,4096]{1,0:T(8,128)(2,1)} %bitcast.21, ...), custom_call_target="tpu_custom_call" | custom-call | tf_op jit(solution)/shard_map/pallas_call | solution.py:763
  119.8 5.5 %shard_map.163 = (bf16[192,2048]{1,0:T(8,128)(2,1)}, bf16[192,4096]{1,0:T(8,128)(2,1)}, bf16[192,4096]{1,0:T(8,128)(2,1)}, bf16[192,256]{1,0:T(8,128)(2,1)}, bf1...) custom-call(bf16[192,2048]{1,0:T(8,128)(2,1)} %get-tuple-element.21.refs_0_, ...), custom_call_target="tpu_custom_call" | custom-call | tf_op jit(solution)/shard_map/pallas_call | solution.py:773

commit v5 on v4

--- a/solution.py
+++ b/solution.py
@@ -398,6 +398,37 @@
     arrived("n4")
     share("s14", 1 - yh, z_far, theirs)
 
+    arrived("s10", "s14")
+    project_back(1 - yh, z_far)
+
+    inner = jnp.sum(acc_ref[...], axis=1, keepdims=True) * (1.0 / E)
+    scaled = r * r * inner
+
+    def gate_back(g, _):
+        base = pl.multiple_of(g * EG, EG)
+        grown = jnp.exp2(lg_ref[g])
+        for p in range(HG // 2):
+            lanes = pl.ds(pl.multiple_of(base + p * 128, 128), 128)
+            zf = z_ref[:, lanes].astype(f32)
+            sig = jax.nn.sigmoid(zf)
+            silu = zf * sig
+            out = y_ref[:, lanes] + pair(skip_ref[g], p, low1) * x_ref[:, lanes].astype(f32)
+            dg = dn_ref[:, lanes].astype(f32) * gain_ref[:, lanes]
+            d_gated = r * (dg - wide_ref[:, lanes] * scaled)
+            dz_ref[:, lanes] = (d_gated * out * (sig * (1.0 + zf * (1.0 - sig)))).astype(bf16)
+            dy = d_gated * silu
+            dy_ref[:, lanes] = dy.astype(bf16)
+            dyel_ref[:, lanes] = (dy * pair(grown, p, low)).astype(bf16)
+        lanes = pl.ds(base, EG)
+        gext_ref[:, lanes] = dot_tn(cg_ref[g], dyel_ref[:, lanes]).astype(bf16)
+        return 0
+
+    lax.fori_loop(0, G, gate_back, 0)
+    dz_copy = pltpu.make_async_copy(dz_ref, dz_out, local_sem.at[7])
+    dz_copy.start()
+    start_all(rev_out)
+    gmine_ref[ctx] = gext_ref[:, lanes_of(ctx)]
+
     for part in range(2):
         for side in range(2):
             hand_cot(part, side).wait_recv()
@@ -436,14 +467,14 @@
 
     y = 2 * yh + yl
     part_width = half_width // 2
-    y_span = part_width // 4
-    z_span = part_width - y_span
-
-    def y_first(part, start=0):
-        return pl.ds(part * start + part * (0 if start else y_span), y_span)
-
-    def z_first(part, start=0):
-        return pl.ds(part * start + (y_span if start else part * z_span), z_span)
+    y_spans = (part_width // 4, part_width // 2)
+    z_spans = tuple(part_width - n for n in y_spans)
+
+    def y_first(part, whole=False):
+        return pl.ds(part * part_width if whole else part * y_spans[0], y_spans[part])
+
+    def z_first(part, whole=False):
+        return pl.ds(part * part_width + y_spans[part] if whole else part * z_spans[0], z_spans[part])
 
     def rows_of(yl_):
         return pl.ds(pl.multiple_of(yl_ * 64, 64), 64)
@@ -459,10 +490,10 @@
         copies = []
         for k in (1, 3, 2):
             yh_, yl_ = along_y(k)
-            copies.append(reduce_copy(12 * part + k - 1, own_ref.at[yh_, :, rows_of(yl_), y_first(part, part_width)],
+            copies.append(reduce_copy(12 * part + k - 1, own_ref.at[yh_, :, rows_of(yl_), y_first(part, True)],
                                       ra1_ref.at[y, :, :, y_first(part)], dev(yh_=yh_, yl_=yl_)))
             z_ = (z + k) % NZ
-            copies.append(reduce_copy(12 * part + k + 2, own_ref.at[:, z_, :, z_first(part, part_width)],
+            copies.append(reduce_copy(12 * part + k + 2, own_ref.at[:, z_, :, z_first(part, True)],
                                       rb1_ref.at[z, :, :, z_first(part)], dev(z_=z_)))
         for cp in copies:
             cp.start()
@@ -518,8 +549,8 @@
     def spread_sum(part):
         for cp in step2[part]:
             cp.wait_recv()
-        piece_ref[:, y_first(part, part_width)] = total_of(ra2_ref, y_first(part))
-        piece_ref[:, z_first(part, part_width)] = total_of(rb2_ref, z_first(part))
+        piece_ref[:, y_first(part, True)] = total_of(ra2_ref, y_first(part))
+        piece_ref[:, z_first(part, True)] = total_of(rb2_ref, z_first(part))
         for k in (2, 6, 4, 1, 3, 7, 5, 0):
             send_sum(k, part).start()
         own_piece(part).start()
@@ -531,39 +562,9 @@
 
     step1 = [first_step(0), first_step(1)]
     for part in range(2):
-        ra1_ref[y, :, :, y_first(part)] = own_ref[yh, :, rows_of(yl), y_first(part, part_width)]
-        rb1_ref[z, :, :, z_first(part)] = own_ref[:, z, :, z_first(part, part_width)]
-
-    arrived("s10", "s14")
-    project_back(1 - yh, z_far)
-
-    inner = jnp.sum(acc_ref[...], axis=1, keepdims=True) * (1.0 / E)
-    scaled = r * r * inner
-
-    def gate_back(g, _):
-        base = pl.multiple_of(g * EG, EG)
-        grown = jnp.exp2(lg_ref[g])
-        for p in range(HG // 2):
-            lanes = pl.ds(pl.multiple_of(base + p * 128, 128), 128)
-            zf = z_ref[:, lanes].astype(f32)
-            sig = jax.nn.sigmoid(zf)
-            silu = zf * sig
-            out = y_ref[:, lanes] + pair(skip_ref[g], p, low1) * x_ref[:, lanes].astype(f32)
-            dg = dn_ref[:, lanes].astype(f32) * gain_ref[:, lanes]
-            d_gated = r * (dg - wide_ref[:, lanes] * scaled)
-            dz_ref[:, lanes] = (d_gated * out * (sig * (1.0 + zf * (1.0 - sig)))).astype(bf16)
-            dy = d_gated * silu
-            dy_ref[:, lanes] = dy.astype(bf16)
-            dyel_ref[:, lanes] = (dy * pair(grown, p, low)).astype(bf16)
-        lanes = pl.ds(base, EG)
-        gext_ref[:, lanes] = dot_tn(cg_ref[g], dyel_ref[:, lanes]).astype(bf16)
-        return 0
-
-    lax.fori_loop(0, G, gate_back, 0)
-    dz_copy = pltpu.make_async_copy(dz_ref, dz_out, local_sem.at[7])
-    dz_copy.start()
-    start_all(rev_out)
-    gmine_ref[ctx] = gext_ref[:, lanes_of(ctx)]
+        ra1_ref[y, :, :, y_first(part)] = own_ref[yh, :, rows_of(yl), y_first(part, True)]
+        rb1_ref[z, :, :, z_first(part)] = own_ref[:, z, :, z_first(part, True)]
+
     project_out(1 - yh, z_far)
     out_ref[...] = lay_ref[...].astype(bf16)
     layer_copy = pltpu.make_async_copy(out_ref, layer_ref, local_sem.at[6])
@@ -615,15 +616,14 @@
         return 0
 
     lax.fori_loop(0, G // 2, within_back, 0)
-    step2 = [second_step(0)]
-    lax.fori_loop(G // 2, G, within_back, 0)
     wait_recv_all(rev_out)
     wait_send_all(fwd_back)
     link(True, gmine_ref, link_ref, reach_ref)
     start_all(rev_back)
-
-    step2.append(second_step(1))
+    step2 = [second_step(0)]
+    lax.fori_loop(G // 2, G, within_back, 0)
     spread_sum(0)
+
     wait_recv_all(rev_back)
 
     def finish(g, _):
@@ -658,10 +658,11 @@
         qs_ref[G + g] += q2
         return 0
 
+    step2.append(second_step(1))
     lax.fori_loop(0, G // 2, finish, 0)
     spread_sum(1)
+    hand_all(0)
     lax.fori_loop(G // 2, G, finish, 0)
-    hand_all(0)
     dx_out = pltpu.make_async_copy(dy_ref, dx_ref, local_sem.at[3])
     dx_out.start()
     a_neg = -jnp.exp(al_ref[...])
@@ -754,8 +755,8 @@
         ((2 * G, rows, HG), f32), ((G, rows, N), f32), group_cols,
         per_group, per_group, ((H, rows), f32), group_cols, group_cols, ((rows, 128), f32), ((G, 1, HG), f32),
         ext, share, linked, state, state, linked, state,
-        ((2, NZ, 128, width // 2), bf16), block, block, ((4, NZ, 64, width // 8), bf16), ((NZ, 2, 128, 3 * width // 8), bf16),
-        ((NZ, 64, width // 8), bf16), ((4, 64, 3 * width // 8), bf16), ((64, width // 2), bf16),
+        ((2, NZ, 128, width // 2), bf16), block, block, ((4, NZ, 64, 3 * width // 16), bf16), ((NZ, 2, 128, 5 * width // 16), bf16),
+        ((NZ, 64, 3 * width // 16), bf16), ((4, 64, 5 * width // 16), bf16), ((64, width // 2), bf16),
     ]
     sems = [9, 36, 36, 8, 8, 3, 3] + [NCTX - 1] * 8 + [NDP // 2, NDP // 2, 24, 24] + [4 * NX] * 4
     vmem = pl.BlockSpec(memory_space=pltpu.VMEM)

time: 126 us -> 130 us (1.032)
  Pallas kernels: 125 us -> 129 us
    pallas_call x1, Pallas kernels: 119 us -> 124 us  [shards(): pl.pallas_call(layer_kernel, out_shape=[jax.ShapeDtypeStruct(s, d) for s,...]
where the time goes in v5:
time: 130 us
  Pallas kernels  129 us (99%)
    pallas_call x1, Pallas kernels, shards(): pl.pallas_call(layer_kernel, out_shape=[jax.ShapeDtypeStruct(s, d) for s,...  124 us
    pallas_call x1, Pallas kernels, shards(): pl.pallas_call(result_kernel, out_shape=[jax.ShapeDtypeStruct(s, d) for s...  5.52 us

profile of v5, /device:TPU:1, one launch (start us, length us, event | category | flops | bytes accessed | tf_op | source)
XLA Modules:
  0.0 129.8 jit_solution(4811064449781365873)
XLA Ops:
  0.6 123.5 %shard_map.162 = (bf16[192,2048]{1,0:T(8,128)(2,1)}, bf16[192,4096]{1,0:T(8,128)(2,1)}, bf16[192,4096]{1,0:T(8,128)(2,1)}, bf16[192,256]{1,0:T(8,128)(2,1)}, bf1...) custom-call(bf16[192,4096]{1,0:T(8,128)(2,1)} %bitcast.20, bf16[192,4096]{1,0:T(8,128)(2,1)} %bitcast.21, ...), custom_call_target="tpu_custom_call" | custom-call | tf_op jit(solution)/shard_map/pallas_call | solution.py:764
  124.2 5.5 %shard_map.163 = (bf16[192,2048]{1,0:T(8,128)(2,1)}, bf16[192,4096]{1,0:T(8,128)(2,1)}, bf16[192,4096]{1,0:T(8,128)(2,1)}, bf16[192,256]{1,0:T(8,128)(2,1)}, bf1...) custom-call(bf16[192,2048]{1,0:T(8,128)(2,1)} %get-tuple-element.21.refs_0_, ...), custom_call_target="tpu_custom_call" | custom-call | tf_op jit(solution)/shard_map/pallas_call | solution.py:774

commit v6 on v5

--- a/solution.py
+++ b/solution.py
@@ -535,6 +535,9 @@
 
     def send_sum(k, part):
         i = 8 * part + k
+        if k % 2 and k > 1:
+            src = place(x, 1 - yl, part)
+            return remote(src, src, p_send.at[i], p_recv.at[i], dev(x_=(x + k // 2) % NX))
         target = sibling if k == 0 else dev(x_=(x + k // 2) % NX, yl_=(yl + k) % 2)
         return remote(own_cols(part), place(x, yl, part), p_send.at[i], p_recv.at[i], target)
 
@@ -551,13 +554,19 @@
             cp.wait_recv()
         piece_ref[:, y_first(part, True)] = total_of(ra2_ref, y_first(part))
         piece_ref[:, z_first(part, True)] = total_of(rb2_ref, z_first(part))
-        for k in (2, 6, 4, 1, 3, 7, 5, 0):
+        for k in (1, 2, 6, 4, 0):
             send_sum(k, part).start()
         own_piece(part).start()
 
+    def pass_sum(part):
+        send_sum(1, part).wait_recv()
+        for k in (3, 7, 5):
+            send_sum(k, part).start()
+
     def hand_all(part):
-        for k in (2, 6, 1, 3, 7, 4, 5):
-            send_sum(k, part).wait_recv()
+        for k in (1, 2, 6, 4, 3, 7, 5):
+            if k > 1:
+                send_sum(k, part).wait_recv()
             hand_on(k, part).start()
 
     step1 = [first_step(0), first_step(1)]
@@ -620,9 +629,8 @@
     wait_send_all(fwd_back)
     link(True, gmine_ref, link_ref, reach_ref)
     start_all(rev_back)
+    lax.fori_loop(G // 2, G, within_back, 0)
     step2 = [second_step(0)]
-    lax.fori_loop(G // 2, G, within_back, 0)
-    spread_sum(0)
 
     wait_recv_all(rev_back)
 
@@ -659,10 +667,13 @@
         return 0
 
     step2.append(second_step(1))
+    spread_sum(0)
     lax.fori_loop(0, G // 2, finish, 0)
+    pass_sum(0)
     spread_sum(1)
+    lax.fori_loop(G // 2, G, finish, 0)
+    pass_sum(1)
     hand_all(0)
-    lax.fori_loop(G // 2, G, finish, 0)
     dx_out = pltpu.make_async_copy(dy_ref, dx_ref, local_sem.at[3])
     dx_out.start()
     a_neg = -jnp.exp(al_ref[...])

time: 130 us -> 127 us (0.977)
  Pallas kernels: 129 us -> 126 us
    pallas_call x1, Pallas kernels: 124 us -> 120 us  [shards(): pl.pallas_call(layer_kernel, out_shape=[jax.ShapeDtypeStruct(s, d) for s,...]
where the time goes in v6:
time: 127 us
  Pallas kernels  126 us (99%)
    pallas_call x1, Pallas kernels, shards(): pl.pallas_call(layer_kernel, out_shape=[jax.ShapeDtypeStruct(s, d) for s,...  120 us
    pallas_call x1, Pallas kernels, shards(): pl.pallas_call(result_kernel, out_shape=[jax.ShapeDtypeStruct(s, d) for s...  5.52 us

profile of v6, /device:TPU:1, one launch (start us, length us, event | category | flops | bytes accessed | tf_op | source)
XLA Modules:
  0.0 126.7 jit_solution(15715760593828952835)
XLA Ops:
  0.6 120.3 %shard_map.162 = (bf16[192,2048]{1,0:T(8,128)(2,1)}, bf16[192,4096]{1,0:T(8,128)(2,1)}, bf16[192,4096]{1,0:T(8,128)(2,1)}, bf16[192,256]{1,0:T(8,128)(2,1)}, bf1...) custom-call(bf16[192,4096]{1,0:T(8,128)(2,1)} %bitcast.20, bf16[192,4096]{1,0:T(8,128)(2,1)} %bitcast.21, ...), custom_call_target="tpu_custom_call" | custom-call | tf_op jit(solution)/shard_map/pallas_call | solution.py:775
  121.0 5.5 %shard_map.163 = (bf16[192,2048]{1,0:T(8,128)(2,1)}, bf16[192,4096]{1,0:T(8,128)(2,1)}, bf16[192,4096]{1,0:T(8,128)(2,1)}, bf16[192,256]{1,0:T(8,128)(2,1)}, bf1...) custom-call(bf16[192,2048]{1,0:T(8,128)(2,1)} %get-tuple-element.21.refs_0_, ...), custom_call_target="tpu_custom_call" | custom-call | tf_op jit(solution)/shard_map/pallas_call | solution.py:785

commit v7 on v4

--- a/solution.py
+++ b/solution.py
@@ -504,6 +504,9 @@
 
     def send_sum(k, part):
         i = 8 * part + k
+        if part == 0 and k in (3, 5, 7):
+            src = place(x, 1 - yl, part)
+            return remote(src, src, p_send.at[i], p_recv.at[i], dev(x_=(x + k // 2) % NX))
         target = sibling if k == 0 else dev(x_=(x + k // 2) % NX, yl_=(yl + k) % 2)
         return remote(own_cols(part), place(x, yl, part), p_send.at[i], p_recv.at[i], target)
 
@@ -520,13 +523,19 @@
             cp.wait_recv()
         piece_ref[:, y_first(part, part_width)] = total_of(ra2_ref, y_first(part))
         piece_ref[:, z_first(part, part_width)] = total_of(rb2_ref, z_first(part))
-        for k in (2, 6, 4, 1, 3, 7, 5, 0):
+        for k in (1, 2, 6, 4, 0) if part == 0 else (2, 6, 4, 1, 3, 7, 5, 0):
             send_sum(k, part).start()
         own_piece(part).start()
 
+    def pass_sum():
+        send_sum(1, 0).wait_recv()
+        for k in (3, 7, 5):
+            send_sum(k, 0).start()
+
     def hand_all(part):
         for k in (2, 6, 1, 3, 7, 4, 5):
-            send_sum(k, part).wait_recv()
+            if part == 1 or k != 1:
+                send_sum(k, part).wait_recv()
             hand_on(k, part).start()
 
     step1 = [first_step(0), first_step(1)]
@@ -659,6 +668,7 @@
         return 0
 
     lax.fori_loop(0, G // 2, finish, 0)
+    pass_sum()
     spread_sum(1)
     lax.fori_loop(G // 2, G, finish, 0)
     hand_all(0)

time: 126 us -> 127 us (level)
  no operation moved by 1% of the time
where the time goes in v7:
time: 127 us
  Pallas kernels  126 us (99%)
    pallas_call x1, Pallas kernels, shards(): pl.pallas_call(layer_kernel, out_shape=[jax.ShapeDtypeStruct(s, d) for s,...  120 us
    pallas_call x1, Pallas kernels, shards(): pl.pallas_call(result_kernel, out_shape=[jax.ShapeDtypeStruct(s, d) for s...  5.52 us

profile of v7, /device:TPU:1, one launch (start us, length us, event | category | flops | bytes accessed | tf_op | source)
XLA Modules:
  0.0 126.5 jit_solution(12603708787786808641)
XLA Ops:
  0.6 120.2 %shard_map.162 = (bf16[192,2048]{1,0:T(8,128)(2,1)}, bf16[192,4096]{1,0:T(8,128)(2,1)}, bf16[192,4096]{1,0:T(8,128)(2,1)}, bf16[192,256]{1,0:T(8,128)(2,1)}, bf1...) custom-call(bf16[192,4096]{1,0:T(8,128)(2,1)} %bitcast.20, bf16[192,4096]{1,0:T(8,128)(2,1)} %bitcast.21, ...), custom_call_target="tpu_custom_call" | custom-call | tf_op jit(solution)/shard_map/pallas_call | solution.py:773
  120.8 5.5 %shard_map.163 = (bf16[192,2048]{1,0:T(8,128)(2,1)}, bf16[192,4096]{1,0:T(8,128)(2,1)}, bf16[192,4096]{1,0:T(8,128)(2,1)}, bf16[192,256]{1,0:T(8,128)(2,1)}, bf1...) custom-call(bf16[192,2048]{1,0:T(8,128)(2,1)} %get-tuple-element.21.refs_0_, ...), custom_call_target="tpu_custom_call" | custom-call | tf_op jit(solution)/shard_map/pallas_call | solution.py:783
